TPU v7x, 256 devices: a whole 4x4x8 slice. The times are simulated.
256 devices in a mesh: blk: 64 (over y_hi, z, x), head: 4 (over y_lo, core).
Axes of the slice: x: 4, y: 4 (y_hi: 2, y_lo: 2; y = y_hi * 2 + y_lo), z: 8, core: 2. Of those that a mesh axis runs over, the one named last changes fastest.
Arguments:
- queries: bfloat16 [32768, 1024], P(('blk', 'head')), may hold values from -5.25 to 5.25
- keys: bfloat16 [32768, 1024], P(('blk', 'head')), may hold values from -5.25 to 5.25
- values: bfloat16 [32768, 1024], P(('blk', 'head')), may hold values from -5 to 5
- out_grad: bfloat16 [32768, 1024], P(('blk', 'head')), may hold values from -5 to 5
- node_order: int32 [32768], P('blk'), may hold values from 0 to 511, as said below
- block_lists: int32 [256, 12], P('blk'), may hold values from 0 to 19, as said below
- block_counts: int32 [256], P('blk'), may hold values from 1 to 12
Outputs:
- attn_out: bfloat16 [32768, 1024], P(('blk', 'head'))
- query_grad: bfloat16 [32768, 1024], P(('blk', 'head'))
- key_grad: bfloat16 [32768, 1024], P(('blk', 'head'))
- value_grad: bfloat16 [32768, 1024], P(('blk', 'head'))
Inputs may be any that keep to these rules, and one draw needn't show every extreme that they name: `node_order`: within each aligned block of 512 entries, every number of 0 to 511 stands once. `block_lists`: the entries of a row are distinct; the first is the block's own entry 8 + g % 4.
All inputs are finite; a program needn't handle non-finite values.
Results may differ from a plain program's by a relative error of at most 0.035.
Values may be sent and summed in bfloat16 or wider, within the bound.
A program may use at most 192 MiB of HBM per device.

v0:
```python
import math

import jax
import jax.numpy as jnp
from jax import lax
from jax.sharding import PartitionSpec as P

HEAD_DIM = 64
LIST = 12


def from_behind(block, axis, distance):
    devices = range(lax.axis_size(axis))
    route = [((i - distance) % len(devices), i) for i in devices]
    return lax.ppermute(block, axis, route)


def fetch_part(own_pair, offset):
    return from_behind(own_pair, "blk", offset)


def return_part(partial_value, offset):
    return from_behind(partial_value, "blk", offset)


def body(queries, keys, values, out_grad, node_order, block_lists, block_counts):
    spread = (
        lax.all_to_all(queries, "head", split_axis=1, concat_axis=0, tiled=True),
        lax.all_to_all(keys, "head", split_axis=1, concat_axis=0, tiled=True),
        lax.all_to_all(values, "head", split_axis=1, concat_axis=0, tiled=True),
        lax.all_to_all(out_grad, "head", split_axis=1, concat_axis=0, tiled=True),
    )
    seg_rows = spread[0].shape[0]
    blocks = block_lists.shape[0]
    blk_rows = seg_rows // blocks
    feat_width = spread[0].shape[1]
    heads_here = feat_width // HEAD_DIM
    key_span = LIST * blk_rows
    score_scale = 1.0 / math.sqrt(HEAD_DIM)
    inverse = jnp.zeros_like(node_order).at[node_order].set(jnp.arange(seg_rows, dtype=jnp.int32))
    query_rows, key_rows, value_rows, grad_rows = [
        jnp.take(member, node_order, axis=0) for member in spread
    ]
    own_pair = jnp.stack((key_rows, value_rows))
    window_parts = [
        own_pair if offset == 0 else fetch_part(own_pair, -offset) for offset in (-2, -1, 0, 1, 2)
    ]
    window = jnp.concatenate(window_parts, axis=1).reshape(2, 5 * blocks, blk_rows, feat_width)
    group_size = min(blocks, max(1, 512 // blk_rows))
    groups = blocks // group_size
    query_groups = query_rows.reshape(groups, group_size, blk_rows, heads_here, HEAD_DIM)
    grad_groups = grad_rows.reshape(groups, group_size, blk_rows, heads_here, HEAD_DIM)
    entry_groups = block_lists.reshape(groups, group_size, LIST)
    count_groups = block_counts.reshape(groups, group_size)
    slot_of = jnp.arange(key_span, dtype=jnp.int32) // blk_rows

    def one_group(totals, inputs):
        query_block, grad_block, entries, live_count = inputs
        gathered = jnp.take(window, entries, axis=1)
        key_block = gathered[0].reshape(group_size, key_span, heads_here, HEAD_DIM)
        value_block = gathered[1].reshape(group_size, key_span, heads_here, HEAD_DIM)
        scores = (
            jnp.einsum(
                "gqhd,gkhd->ghqk", query_block, key_block, preferred_element_type=jnp.float32
            )
            * score_scale
        )
        is_live = slot_of[None, :] < live_count[:, None]
        scores = jnp.where(is_live[:, None, None, :], scores, -jnp.inf)
        row_max = jnp.max(scores, axis=-1, keepdims=True)
        shifted = jnp.exp(scores - row_max)
        row_total = jnp.sum(shifted, axis=-1, keepdims=True)
        chance = shifted / row_total
        chance_low = chance.astype(jnp.bfloat16)
        attended = jnp.einsum(
            "ghqk,gkhd->gqhd", chance_low, value_block, preferred_element_type=jnp.float32
        ).astype(jnp.bfloat16)
        inner_dot = jnp.einsum(
            "gqhd,gqhd->ghq", grad_block, attended, preferred_element_type=jnp.float32
        )
        grad_chance = jnp.einsum(
            "gqhd,gkhd->ghqk", grad_block, value_block, preferred_element_type=jnp.float32
        )
        grad_score = chance * (grad_chance - inner_dot[..., None])
        grad_low = grad_score.astype(jnp.bfloat16)
        query_part = (
            jnp.einsum("ghqk,gkhd->gqhd", grad_low, key_block, preferred_element_type=jnp.float32)
            * score_scale
        ).astype(jnp.bfloat16)
        key_part = jnp.einsum(
            "ghqk,gqhd->gkhd", grad_low, query_block, preferred_element_type=jnp.float32
        )
        value_part = jnp.einsum(
            "ghqk,gqhd->gkhd", chance_low, grad_block, preferred_element_type=jnp.float32
        )
        stacked = jnp.stack((key_part, value_part)).reshape(
            2, group_size, LIST, blk_rows, feat_width
        )
        totals = totals.at[:, entries].add(stacked)
        row_stats = jnp.stack((row_max[..., 0], row_total[..., 0], inner_dot), axis=1)
        return (totals, (attended, query_part, row_stats))

    start_sum = jnp.zeros((2, 5 * blocks, blk_rows, feat_width), jnp.float32)
    totals, (attended, query_part, stat_groups) = lax.scan(
        one_group, start_sum, (query_groups, grad_groups, entry_groups, count_groups)
    )
    partial_value = totals.reshape(2, 5, seg_rows, feat_width)
    returned = partial_value[:, 2]
    for offset in (-2, -1, 1, 2):
        returned = returned + return_part(partial_value[:, offset + 2], offset)
    key_low = (returned[0] * score_scale).astype(jnp.bfloat16)
    value_low = returned[1].astype(jnp.bfloat16)
    attended_rows = attended.reshape(seg_rows, feat_width)
    query_low = query_part.reshape(seg_rows, feat_width)
    restored = [
        jnp.take(member, inverse, axis=0)
        for member in (attended_rows, query_low, key_low, value_low)
    ]
    final_parts = (
        lax.all_to_all(restored[0], "head", split_axis=0, concat_axis=1, tiled=True),
        lax.all_to_all(restored[1], "head", split_axis=0, concat_axis=1, tiled=True),
        lax.all_to_all(restored[2], "head", split_axis=0, concat_axis=1, tiled=True),
        lax.all_to_all(restored[3], "head", split_axis=0, concat_axis=1, tiled=True),
    )
    return (final_parts[0], final_parts[1], final_parts[2], final_parts[3])


def solution(mesh):
    in_specs = (
        P(("blk", "head"), None),
        P(("blk", "head"), None),
        P(("blk", "head"), None),
        P(("blk", "head"), None),
        P("blk"),
        P("blk", None),
        P("blk"),
    )
    out_specs = (
        P(("blk", "head"), None),
        P(("blk", "head"), None),
        P(("blk", "head"), None),
        P(("blk", "head"), None),
    )
    return jax.shard_map(body, mesh=mesh, in_specs=in_specs, out_specs=out_specs, check_vma=False)
```

profile of v0, /device:TPU:102, one launch (start us, length us, event | category | flops | bytes accessed | tf_op | source)
XLA Modules:
  0.0 382.0 jit_solution(4664651699061886196)
XLA Ops:
  0.6 1.7 copy.84
  2.3 3.4 all-to-all-start.2
  6.5 1.7 copy.86
  8.1 3.6 all-to-all-done.2
  11.7 3.4 all-to-all-start
  15.8 1.7 copy.85
  17.5 1.7 copy.83
  19.2 2.0 all-to-all-done
  21.1 3.4 all-to-all-start.1
  25.2 5.3 %all-to-all-done.1 = bf16[128,4,256]{2,0,1:T(8,128)(2,1)S(1)} async-done(((bf16[128,4,256]{2,0,1:T(8,128)(2,1)}), bf16[128,4,256]{2,0,1:T(8,128)(2,1)S(1)}, u32[]{:S(2)}, u32[]{:S(2)}) %all-to-all-start.1) | async-done | bytes 262176 | tf_op jit(solution)/shard_map/all_to_all | solution.py:30
  30.6 3.4 all-to-all-start.4
  34.7 1.9 gather_fusion.3
  36.6 2.0 gather_fusion.1
  38.6 2.0 gather_fusion.2
  40.5 2.0 gather_fusion.5
  43.5 3.0 collective-permute-start.1
  46.6 2.4 collective-permute-start
  49.1 2.4 scatter_custom_fusion
  51.5 1.2 collective-permute-start.3
  55.1 26.5 %collective-permute-done = bf16[2,512,256]{2,1,0:T(8,128)(2,1)} collective-permute-done((bf16[2,512,256]{2,1,0:T(8,128)(2,1)}, bf16[2,512,256]{2,1,0:T(8,128)(2,1)}, u32[]{:S(2)}, u32[]{:S(2)}) %collective-permute-start) | collective-permute-done | bytes 524320 | tf_op jit(solution)/shard_map/ppermute | solution.py:15
  81.5 1.1 constant_dynamic-update-slice_fusion.4
  82.6 1.1 constant_dynamic-update-slice_fusion.3
  83.7 3.1 collective-permute-done.2
  87.9 1.1 constant_dynamic-update-slice_fusion
  89.0 5.2 %gather_fusion = bf16[48,2,128,256]{3,2,1,0:T(8,128)(2,1)} fusion(bf16[2,20,128,256]{3,2,1,0:T(8,128)(2,1)S(1)} %bitcast.135, s32[1024]{0:T(1024)S(1)} %pad_clamp_fusion.1), kind=kCustom, calls=%fused_computation.8 | custom fusion | bytes 12583104 | tf_op jit(solution)/shard_map/while/body/eval_jaxpr/jit(_take)/gather | solution.py:59
  94.1 3.4 select_bitcast_fusion
  97.6 2.1 fusion.26
  99.7 5.5 %copy.28 = bf16[1,4,12,128,256]{3,2,4,1,0:T(8,128)(2,1)} copy(bf16[1,4,12,128,256]{4,3,0,2,1:T(8,128)(2,1)S(1)} %get-tuple-element.25) | data formatting | bytes 6291456 | tf_op jit(solution)/shard_map/while/body/eval_jaxpr/slice | solution.py:60
  105.3 5.5 %squeeze.42 = bf16[4,1536,4,64]{1,3,2,0:T(8,128)(2,1)S(1)} reshape(bf16[1,4,12,128,256]{3,2,4,1,0:T(8,128)(2,1)} %copy.28) | data formatting | bytes 6291456 | tf_op jit(solution)/shard_map/while/body/eval_jaxpr/reshape;while/body/eval_jaxpr/squeeze | solution.py:60
  110.8 7.7 %copy.25 = bf16[1,4,12,128,256]{3,2,4,1,0:T(8,128)(2,1)} copy(bf16[1,4,12,128,256]{4,3,0,2,1:T(8,128)(2,1)} %get-tuple-element.26) | data formatting | bytes 6291456 | tf_op jit(solution)/shard_map/while/body/eval_jaxpr/slice | solution.py:61
  118.5 6.9 %squeeze.40 = bf16[4,1536,4,64]{1,3,2,0:T(8,128)(2,1)} reshape(bf16[1,4,12,128,256]{3,2,4,1,0:T(8,128)(2,1)} %copy.25) | data formatting | bytes 6291456 | tf_op jit(solution)/shard_map/while/body/eval_jaxpr/reshape;while/body/eval_jaxpr/squeeze | solution.py:61
  125.3 6.6 %fusion.27 = (f32[4,4,128]{2,1,0:T(4,128)S(1)}, f32[4,4,128,1536]{3,2,1,0:T(8,128)}) fusion(pred[4,1536]{1,0:T(4,128)(4,1)S(1)} %broadcast_compare_fusion, bf16[4,128,4,64]{1,3,2,0:T(8,128)(2,1)S(1)} %copy-done.6, bf16[4,1536,4,64]{1,3,2,0:T(8,128)(2,1)S(1)} %squeeze.42), kind=kOutput, calls=%fused_computation.88 | convolution fusion | flops 415237632 | bytes 16005120 | tf_op jit(solution)/shard_map/while/body/eval_jaxpr/sub | solution.py:71
  131.9 8.9 %fusion.5 = bf16[4,4,128,1536]{3,2,1,0:T(8,128)(2,1)} fusion(f32[4,4,128,1536]{3,2,1,0:T(8,128)} %get-tuple-element.50, f32[4,4,128]{2,1,0:T(4,128)S(1)} %get-tuple-element.49), kind=kLoop, calls=%fused_computation.22 | loop fusion | flops 6291456 | bytes 18882560 | tf_op jit(solution)/shard_map/while/body/eval_jaxpr/convert_element_type | solution.py:74
  140.9 6.9 %convolution_bitcast_fusion = f32[4,1536,4,64]{1,3,2,0:T(8,128)} fusion(bf16[4,4,128,1536]{3,2,1,0:T(8,128)(2,1)} %fusion.5, bf16[4,128,4,64]{1,0,3,2:T(4,128)(2,1)S(1)} %copy-done.5), kind=kOutput, calls=%fused_computation.23 | convolution fusion | flops 402653184 | bytes 12845056 | tf_op jit(solution)/shard_map/while/body/eval_jaxpr/ghqk,gqhd->gkhd/dot_general | solution.py:93
  148.2 2.3 multiply_reduce_fusion
  150.5 5.9 %multiply_convert_fusion = bf16[4,4,128,1536]{3,2,1,0:T(8,128)(2,1)S(1)} fusion(bf16[4,1536,4,64]{1,3,2,0:T(8,128)(2,1)S(1)} %copy-done.2, f32[4,4,128]{2,1,0:T(4,128)S(1)} %get-tuple-element.51, f32[4,4,128,1536]{3,2,1,0:T(8,128)} %get-tuple-element.50, f32[4,4,128]{2,1,0:T(4,128)S(1)} %get-tuple-element.49, bf16[4,128,4,64]{1,0,3,2:T(4,128)(2,1)S(1)} %copy-done.5), kind=kOutput, calls=%fused_computation.13 | convolution fusion | flops 415236096 | bytes 22298624 | tf_op jit(solution)/shard_map/while/body/eval_jaxpr/gqhd,gkhd->ghqk/dot_general | solution.py:81
  156.4 2.6 copy-done.1
  159.0 3.7 convolution_bitcast_fusion.1
  162.7 8.4 %stack.24 = f32[1,4,12,128,256]{3,2,4,1,0:T(8,128)} reshape(f32[4,1536,4,64]{1,3,2,0:T(8,128)} %convolution_bitcast_fusion.1) | data formatting | bytes 12582912 | tf_op jit(solution)/shard_map/while/body/eval_jaxpr/stack | solution.py:96
  171.1 8.4 %stack.25 = f32[1,4,12,128,256]{3,2,4,1,0:T(8,128)} reshape(f32[4,1536,4,64]{1,3,2,0:T(8,128)} %convolution_bitcast_fusion) | data formatting | bytes 12582912 | tf_op jit(solution)/shard_map/while/body/eval_jaxpr/stack | solution.py:96
  179.5 11.3 %maximum_bitcast_fusion = f32[4,12,2,128,256]{3,1,4,0,2:T(8,128)} fusion(f32[1,4,12,128,256]{3,2,4,1,0:T(8,128)} %stack.25, f32[1,4,12,128,256]{3,2,4,1,0:T(8,128)} %stack.24), kind=kLoop, calls=%fused_computation.12 | loop fusion | flops 3145728 | bytes 25165824 | tf_op jit(solution)/shard_map/while/body/eval_jaxpr/stack | solution.py:96
  190.8 17.6 %copy.41 = f32[4,12,2,128,256]{4,3,2,1,0:T(8,128)} copy(f32[4,12,2,128,256]{3,1,4,0,2:T(8,128)} %maximum_bitcast_fusion) | data formatting | bytes 25165824 | tf_op jit(solution)/shard_map/while/body/eval_jaxpr/stack | solution.py:96
  208.4 2.9 broadcast_in_dim.70
  211.4 28.0 %scatter_fusion = f32[2,20,128,256]{3,2,1,0:T(8,128)} fusion(f32[2,20,128,256]{3,2,1,0:T(8,128)} %broadcast_in_dim.70, s32[48]{0:T(128)S(1)} %reshape.186, f32[48,2,128,256]{3,2,1,0:T(8,128)} %bitcast.129), kind=kCustom, calls=%fused_computation.10 | custom fusion | flops 3145728 | bytes 37748928 | tf_op jit(solution)/shard_map/while/body/eval_jaxpr/scatter-add | solution.py:99
  239.4 4.4 %slice_bitcast_fusion.3 = (f32[2,512,256]{2,1,0:T(8,128)}, f32[2,512,256]{2,1,0:T(8,128)}, f32[2,512,256]{2,1,0:T(8,128)}, f32[2,512,256]{2,1,0:T(8,128)}) fusion(f32[2,5,512,256]{3,2,1,0:T(8,128)} %bitcast.127), kind=kLoop, calls=%fused_computation.33 | loop fusion | bytes 8388608 | tf_op jit(solution)/shard_map/squeeze | solution.py:110
  243.8 3.1 collective-permute-start.4
  246.9 4.0 %collective-permute-start.6 = (f32[2,512,256]{2,1,0:T(8,128)}, f32[2,512,256]{2,1,0:T(8,128)}, u32[]{:S(2)}, u32[]{:S(2)}) collective-permute-start(f32[2,512,256]{2,1,0:T(8,128)} %get-tuple-element.28), channel_id=1, source_target_pairs={{252,0},{0,4},{4,8},{8,12},{12,16},{16,20},{20,24},{24,28},{28,32}... | collective-permute-start | bytes 3145736 | tf_op jit(solution)/shard_map/ppermute | solution.py:15
  251.0 1.5 collective-permute-start.7
  252.4 1.1 copy.55
  253.5 1.5 reshape.240
  255.0 5.7 %fusion.7 = bf16[4,128,4,64]{1,3,2,0:T(8,128)(2,1)} fusion(bf16[4,1536,4,64]{1,3,2,0:T(8,128)(2,1)S(1)} %squeeze.42, bf16[4,4,128,1536]{3,2,1,0:T(8,128)(2,1)} %copy-done.1), kind=kOutput, calls=%fused_computation.28 | convolution fusion | flops 402915328 | bytes 9699328 | tf_op jit(solution)/shard_map/while/body/eval_jaxpr/ghqk,gkhd->gqhd/dot_general | solution.py:87
  260.7 1.2 copy.56
  262.3 2.0 gather_fusion.4
  264.3 2.0 gather_fusion.6
  266.3 6.0 %collective-permute-done.4 = f32[2,512,256]{2,1,0:T(8,128)} collective-permute-done((f32[2,512,256]{2,1,0:T(8,128)}, f32[2,512,256]{2,1,0:T(8,128)}, u32[]{:S(2)}, u32[]{:S(2)}) %collective-permute-start.4) | collective-permute-done | bytes 1048608 | tf_op jit(solution)/shard_map/ppermute | solution.py:15
  272.2 66.7 %collective-permute-done.6 = f32[2,512,256]{2,1,0:T(8,128)} collective-permute-done((f32[2,512,256]{2,1,0:T(8,128)}, f32[2,512,256]{2,1,0:T(8,128)}, u32[]{:S(2)}, u32[]{:S(2)}) %collective-permute-start.6) | collective-permute-done | bytes 1048608 | tf_op jit(solution)/shard_map/ppermute | solution.py:15
  338.9 2.8 fusion.13
  341.8 2.0 gather_fusion.7
  343.8 2.0 gather_fusion.8
  346.6 8.4 %all_to_all.152 = bf16[4,128,256]{2,1,0:T(8,128)(2,1)S(1)} all-to-all(bf16[4,128,256]{2,1,0:T(8,128)(2,1)S(1)} %bitcast.139), channel_id=1, replica_groups=mesh['blk'=64,'head'=4] {'head'}, dimensions={0} | all-to-all | bytes 524288 | tf_op jit(solution)/shard_map/all_to_all | solution.py:121
  355.0 8.4 %all_to_all.153 = bf16[4,128,256]{2,1,0:T(8,128)(2,1)S(1)} all-to-all(bf16[4,128,256]{2,1,0:T(8,128)(2,1)S(1)} %bitcast.138), channel_id=1, replica_groups=mesh['blk'=64,'head'=4] {'head'}, dimensions={0} | all-to-all | bytes 524288 | tf_op jit(solution)/shard_map/all_to_all | solution.py:123
  363.5 8.4 %all_to_all.154 = bf16[4,128,256]{2,1,0:T(8,128)(2,1)S(1)} all-to-all(bf16[4,128,256]{2,1,0:T(8,128)(2,1)S(1)} %bitcast.137), channel_id=1, replica_groups=mesh['blk'=64,'head'=4] {'head'}, dimensions={0} | all-to-all | bytes 524288 | tf_op jit(solution)/shard_map/all_to_all | solution.py:122
  371.9 3.4 all-to-all-start.3
  377.5 3.8 all-to-all-done.3
  (54 shorter events, 12.0 us)
Async XLA Ops:
  2.3 9.4 %all-to-all-start.2 = ((bf16[128,4,256]{2,0,1:T(8,128)(2,1)}), bf16[128,4,256]{2,0,1:T(8,128)(2,1)S(1)}, u32[]{:S(2)}, u32[]{:S(2)}) async-start(bf16[128,4,256]{2,0,1:T(8,128)(2,1)} %bitcast.123), calls=%async_computation.2 | async-start | bytes 524288 | tf_op jit(solution)/shard_map/all_to_all | solution.py:28
  11.7 9.4 %all-to-all-start = ((bf16[128,4,256]{2,0,1:T(8,128)(2,1)}), bf16[128,4,256]{2,0,1:T(8,128)(2,1)S(1)}, u32[]{:S(2)}, u32[]{:S(2)}) async-start(bf16[128,4,256]{2,0,1:T(8,128)(2,1)} %bitcast.125), calls=%async_computation | async-start | bytes 524288 | tf_op jit(solution)/shard_map/all_to_all | solution.py:29
  21.1 9.4 %all-to-all-start.1 = ((bf16[128,4,256]{2,0,1:T(8,128)(2,1)}), bf16[128,4,256]{2,0,1:T(8,128)(2,1)S(1)}, u32[]{:S(2)}, u32[]{:S(2)}) async-start(bf16[128,4,256]{2,0,1:T(8,128)(2,1)} %bitcast.124), calls=%async_computation.1 | async-start | bytes 524288 | tf_op jit(solution)/shard_map/all_to_all | solution.py:30
  30.6 10.0 %all-to-all-start.4 = ((bf16[128,4,256]{2,0,1:T(8,128)(2,1)}), bf16[128,4,256]{2,0,1:T(8,128)(2,1)S(1)}, u32[]{:S(2)}, u32[]{:S(2)}) async-start(bf16[128,4,256]{2,0,1:T(8,128)(2,1)} %bitcast.122), calls=%async_computation.4 | async-start | bytes 524288 | tf_op jit(solution)/shard_map/all_to_all | solution.py:31
  34.7 14.3 %copy-start.8 = (s32[4,12]{1,0:T(4,128)S(1)}, s32[4,12]{1,0:T(4,128)}, u32[]{:S(2)}) copy-start(s32[4,12]{1,0:T(4,128)} %param.14) | copy-start | bytes 580
  43.5 39.1 %collective-permute-start.1 = (bf16[2,512,256]{2,1,0:T(8,128)(2,1)}, bf16[2,512,256]{2,1,0:T(8,128)(2,1)}, u32[]{:S(2)}, u32[]{:S(2)}) collective-permute-start(bf16[2,512,256]{2,1,0:T(8,128)(2,1)} %pad_maximum_fusion), channel_id=1, source_target_pairs={{252,0},{0,4},{4,8},{8,12},{12,16},{16,20},{20,24},{24,28},{28,32}... | collective-permute-start | bytes 1572872 | tf_op jit(solution)/shard_map/ppermute | solution.py:15
  46.6 35.0 %collective-permute-start = (bf16[2,512,256]{2,1,0:T(8,128)(2,1)}, bf16[2,512,256]{2,1,0:T(8,128)(2,1)}, u32[]{:S(2)}, u32[]{:S(2)}) collective-permute-start(bf16[2,512,256]{2,1,0:T(8,128)(2,1)} %pad_maximum_fusion), channel_id=1, source_target_pairs={{248,0},{252,4},{0,8},{4,12},{8,16},{12,20},{16,24},{20,28},{24,32... | collective-permute-start | bytes 1572872 | tf_op jit(solution)/shard_map/ppermute | solution.py:15
  51.5 36.4 %collective-permute-start.3 = (bf16[2,512,256]{2,1,0:T(8,128)(2,1)}, bf16[2,512,256]{2,1,0:T(8,128)(2,1)}, u32[]{:S(2)}, u32[]{:S(2)}) collective-permute-start(bf16[2,512,256]{2,1,0:T(8,128)(2,1)} %pad_maximum_fusion), channel_id=1, source_target_pairs={{8,0},{12,4},{16,8},{20,12},{24,16},{28,20},{32,24},{36,28},{40,32... | collective-permute-start | bytes 1572872 | tf_op jit(solution)/shard_map/ppermute | solution.py:15
  52.7 34.1 %collective-permute-start.2 = (bf16[2,512,256]{2,1,0:T(8,128)(2,1)}, bf16[2,512,256]{2,1,0:T(8,128)(2,1)}, u32[]{:S(2)}, u32[]{:S(2)}) collective-permute-start(bf16[2,512,256]{2,1,0:T(8,128)(2,1)} %pad_maximum_fusion), channel_id=1, source_target_pairs={{4,0},{8,4},{12,8},{16,12},{20,16},{24,20},{28,24},{32,28},{36,32}... | collective-permute-start | bytes 1572872 | tf_op jit(solution)/shard_map/ppermute | solution.py:15
  53.0 2.1 copy-start.4
  110.8 14.5 %copy-start.6 = (bf16[4,128,4,64]{1,3,2,0:T(8,128)(2,1)S(1)}, bf16[4,128,4,64]{1,3,2,0:T(8,128)(2,1)}, u32[]{:S(2)}) copy-start(bf16[4,128,4,64]{1,3,2,0:T(8,128)(2,1)} %copy.29) | copy-start | bytes 786436
  131.9 8.9 %copy-start.5 = (bf16[4,128,4,64]{1,0,3,2:T(4,128)(2,1)S(1)}, bf16[4,128,4,64]{1,0,3,2:T(4,128)(2,1)}, u32[]{:S(2)}) copy-start(bf16[4,128,4,64]{1,0,3,2:T(4,128)(2,1)} %copy-done.4) | copy-start | bytes 786436
  140.8 6.9 %copy-start = (bf16[4,4,128,1536]{3,2,1,0:T(8,128)(2,1)S(1)}, bf16[4,4,128,1536]{3,2,1,0:T(8,128)(2,1)}, u32[]{:S(2)}) copy-start(bf16[4,4,128,1536]{3,2,1,0:T(8,128)(2,1)} %fusion.5) | copy-start | bytes 18874372
  140.9 6.9 %copy-start.2 = (bf16[4,1536,4,64]{1,3,2,0:T(8,128)(2,1)S(1)}, bf16[4,1536,4,64]{1,3,2,0:T(8,128)(2,1)}, u32[]{:S(2)}) copy-start(bf16[4,1536,4,64]{1,3,2,0:T(8,128)(2,1)} %squeeze.40) | copy-start | bytes 9437188
  140.9 7.4 %copy-start.3 = (f32[4,4,128,64]{2,0,3,1:T(4,128)S(1)}, f32[4,4,128,64]{2,0,3,1:T(4,128)}, u32[]{:S(2)}) copy-start(f32[4,4,128,64]{2,0,3,1:T(4,128)} %bitcast_convert_fusion) | copy-start | bytes 1572868
  150.5 8.5 %copy-start.7 = (bf16[4,128,4,64]{1,3,2,0:T(8,128)(2,1)S(1)}, bf16[4,128,4,64]{1,3,2,0:T(8,128)(2,1)}, u32[]{:S(2)}) copy-start(bf16[4,128,4,64]{1,3,2,0:T(8,128)(2,1)} %copy.29) | copy-start | bytes 786436
  156.4 2.6 copy-start.1
  243.8 28.4 %collective-permute-start.4 = (f32[2,512,256]{2,1,0:T(8,128)}, f32[2,512,256]{2,1,0:T(8,128)}, u32[]{:S(2)}, u32[]{:S(2)}) collective-permute-start(f32[2,512,256]{2,1,0:T(8,128)} %get-tuple-element.27), channel_id=1, source_target_pairs={{8,0},{12,4},{16,8},{20,12},{24,16},{28,20},{32,24},{36,28},{40,32... | collective-permute-start | bytes 3145736 | tf_op jit(solution)/shard_map/ppermute | solution.py:15
  246.9 92.0 %collective-permute-start.6 = (f32[2,512,256]{2,1,0:T(8,128)}, f32[2,512,256]{2,1,0:T(8,128)}, u32[]{:S(2)}, u32[]{:S(2)}) collective-permute-start(f32[2,512,256]{2,1,0:T(8,128)} %get-tuple-element.28), channel_id=1, source_target_pairs={{252,0},{0,4},{4,8},{8,12},{12,16},{16,20},{20,24},{24,28},{28,32}... | collective-permute-start | bytes 3145736 | tf_op jit(solution)/shard_map/ppermute | solution.py:15
  250.9 88.0 %collective-permute-start.5 = (f32[2,512,256]{2,1,0:T(8,128)}, f32[2,512,256]{2,1,0:T(8,128)}, u32[]{:S(2)}, u32[]{:S(2)}) collective-permute-start(f32[2,512,256]{2,1,0:T(8,128)} %get-tuple-element.29), channel_id=1, source_target_pairs={{4,0},{8,4},{12,8},{16,12},{20,16},{24,20},{28,24},{32,28},{36,32}... | collective-permute-start | bytes 3145736 | tf_op jit(solution)/shard_map/ppermute | solution.py:15
  251.0 88.0 %collective-permute-start.7 = (f32[2,512,256]{2,1,0:T(8,128)}, f32[2,512,256]{2,1,0:T(8,128)}, u32[]{:S(2)}, u32[]{:S(2)}) collective-permute-start(f32[2,512,256]{2,1,0:T(8,128)} %get-tuple-element.40), channel_id=1, source_target_pairs={{248,0},{252,4},{0,8},{4,12},{8,16},{12,20},{16,24},{20,28},{24,32... | collective-permute-start | bytes 3145736 | tf_op jit(solution)/shard_map/ppermute | solution.py:15
  371.9 9.4 %all-to-all-start.3 = ((bf16[4,128,256]{2,1,0:T(8,128)(2,1)}), bf16[4,128,256]{2,1,0:T(8,128)(2,1)S(1)}, u32[]{:S(2)}, u32[]{:S(2)}) async-start(bf16[4,128,256]{2,1,0:T(8,128)(2,1)} %bitcast.14), calls=%async_computation.3 | async-start | bytes 524288 | tf_op jit(solution)/shard_map/all_to_all | solution.py:120
where the time goes:
time: 384 us; the launch traced here: 382 us
  waiting for transfers between devices  117 us (30%)
  local copies, waits for them, and re-layouts  115 us (30%)
  other arithmetic  60.3 us (16%)
  starting transfers between devices  32.3 us (8%)
  matrix products  31.1 us (8%)
  blocking collectives  25.2 us (7%)
    ppermute x8, waiting for transfers between devices, from_behind(): return lax.ppermute(block, axis, route)  102 us
    another operation x3, local copies, waits for them, and re-layouts, one_group(): jnp.stack((key_part, value_part))  34.4 us
    scatter-add x1, other arithmetic, one_group(): totals = totals.at[:, entries].add(stacked)  28 us
    ppermute x8, starting transfers between devices, from_behind(): return lax.ppermute(block, axis, route)  15.3 us
    another operation x1, other arithmetic, one_group(): jnp.stack((key_part, value_part))  11.3 us
    convert_element_type x1, other arithmetic, one_group(): chance_low = chance.astype(jnp.bfloat16)  8.94 us
    all_to_all x1, blocking collectives, body(): lax.all_to_all(restored[3], 'head', split_axis=0, concat_axis=1, tiled=True)  8.41 us
    all_to_all x1, blocking collectives, body(): lax.all_to_all(restored[2], 'head', split_axis=0, concat_axis=1, tiled=True)  8.41 us
  transfers between devices with their start and end apart: 13, of which 8 were waited for; matrix products, arithmetic and copies ran while one was open for 10% of the time, Pallas kernels for 0%

commit v1 on v0

v1 whole, which is shorter than its diff:
```python
import functools
import math

import jax
import jax.numpy as jnp
from jax import lax
from jax.experimental import pallas as pl
from jax.experimental.pallas import tpu as pltpu
from jax.sharding import PartitionSpec as P

BLK = 128
SEG = 512
DIM = 64
LIST = 12
GROUP = 16
NT = (((1,), (1,)), ((), ()))
TN = (((0,), (0,)), ((), ()))
SCALE = 1.0 / math.sqrt(DIM)
LOG2E = math.log2(math.e)
MESH = pl.DeviceIdType.MESH
ANY = pl.BlockSpec(memory_space=pl.ANY)
VMEM = pl.BlockSpec(memory_space=pltpu.VMEM)
SMEM = pl.BlockSpec(memory_space=pltpu.SMEM)


def place():
    blk, head = lax.axis_index("blk"), lax.axis_index("head")
    segs = lax.axis_size("blk")
    quad = blk // 4
    me = (blk % 4) * 4 + head
    left = (lax.rem(blk + segs - 4, segs), head)
    right = (lax.rem(blk + 4, segs), head)
    return quad, me, left, right


def member(quad, slot):
    return (quad * 4 + slot // 4, slot % 4)


def remote(src, dst, ssem, rsem, device):
    return pltpu.make_async_remote_copy(
        src_ref=src, dst_ref=dst, send_sem=ssem, recv_sem=rsem, device_id=device, device_id_type=MESH
    )


def greet(quad, me, left, right):
    barrier = pltpu.get_barrier_semaphore()
    for step in range(1, GROUP):
        pl.semaphore_signal(
            barrier, inc=1, device_id=member(quad, lax.rem(me + step, GROUP)), device_id_type=MESH
        )
    for device in (left, right):
        pl.semaphore_signal(barrier, inc=1, device_id=device, device_id_type=MESH)
    pl.semaphore_wait(barrier, GROUP + 1)


def enter_kernel(
    q_ref, k_ref, v_ref, g_ref, order_ref, lists_ref, counts_ref,
    window_ref, qg_ref, orders_ref, meta_ref,
    kv_out, qg_out, kv_in, qg_in, own_kv, own_qg, order_in, meta_in,
    kv_ss, kv_rs, qg_ss, qg_rs, order_ss, order_rs, meta_ss, meta_rs, halo_ss, halo_rs, local_sem,
):
    quad, me, left, right = place()
    seg = me // 4
    head = me % 4
    meta_in[seg] = jnp.zeros((8, 128), jnp.int32)
    meta_in[seg, 0:4, 0:LIST] = lists_ref[...]
    meta_in[seg, 4:5, 0:4] = counts_ref[...]
    order_in[seg] = order_ref[...]
    for t in range(8):
        cols = slice(t * 128, t * 128 + 128)
        k, v = k_ref[:, cols], v_ref[:, cols]
        kv_out[2 * t] = jnp.concatenate([k[:, :DIM], v[:, :DIM]], axis=1)
        kv_out[2 * t + 1] = jnp.concatenate([k[:, DIM:], v[:, DIM:]], axis=1)
    greet(quad, me, left, right)
    small = []
    for step in range(1, 4):
        peer = member(quad, lax.rem(me + 4 * step, GROUP))
        small.append(remote(order_in.at[seg], order_in.at[seg], order_ss.at[step], order_rs.at[seg], peer))
        small.append(remote(meta_in.at[seg], meta_in.at[seg], meta_ss.at[step], meta_rs.at[seg], peer))
    for copy in small:
        copy.start()
    sends = []
    for step in range(1, GROUP):
        slot = lax.rem(me + step, GROUP)
        sends.append(
            remote(kv_out.at[slot], kv_in.at[me], kv_ss.at[step], kv_rs.at[me], member(quad, slot))
        )
        sends[-1].start()
    kv_in[me] = kv_out[me]
    for t in range(8):
        cols = slice(t * 128, t * 128 + 128)
        q, g = q_ref[:, cols] * SCALE, g_ref[:, cols]
        qg_out[2 * t] = jnp.concatenate([q[:, :DIM], g[:, :DIM]], axis=1)
        qg_out[2 * t + 1] = jnp.concatenate([q[:, DIM:], g[:, DIM:]], axis=1)
    for step in range(1, GROUP):
        slot = lax.rem(me + step, GROUP)
        sends.append(
            remote(qg_out.at[slot], qg_in.at[me], qg_ss.at[step], qg_rs.at[me], member(quad, slot))
        )
        sends[-1].start()
    qg_in[me] = qg_out[me]

    for s in range(4):

        @pl.when(s != seg)
        def _():
            remote(order_in.at[s], order_in.at[s], order_ss.at[0], order_rs.at[s], left).wait_recv()
            remote(meta_in.at[s], meta_in.at[s], meta_ss.at[0], meta_rs.at[s], left).wait_recv()

    def one_hot(s):
        order = jnp.broadcast_to(order_in[s].astype(jnp.float32), (128, SEG))
        order = jnp.transpose(order)
        lane = lax.broadcasted_iota(jnp.int32, (SEG, 128), 1).astype(jnp.float32)
        tiles = [(order == lane + 128.0 * t).astype(jnp.bfloat16) for t in range(4)]
        return jnp.concatenate(tiles, axis=1)

    picks = [one_hot(s) for s in range(4)]
    locals_ = [
        pltpu.make_async_copy(order_in, orders_ref, local_sem.at[8]),
        pltpu.make_async_copy(meta_in, meta_ref, local_sem.at[9]),
    ]
    for copy in locals_:
        copy.start()
    halos = []
    for s in range(4):
        for slot in range(4 * s, 4 * s + 4):

            @pl.when(slot != me)
            def _():
                remote(kv_in.at[slot], kv_in.at[slot], kv_ss.at[0], kv_rs.at[slot], left).wait_recv()

        rows = pl.ds(s * SEG, SEG)
        own_kv[rows, :] = jnp.dot(
            picks[s], kv_in[4 * s : 4 * s + 4].reshape(SEG, 128), preferred_element_type=jnp.float32
        ).astype(jnp.bfloat16)
        there = 3072 + s * SEG if s < 2 else (s - 2) * SEG
        halos.append(
            remote(
                own_kv.at[rows], window_ref.at[pl.ds(there, SEG)], halo_ss.at[s], halo_rs.at[s],
                left if s < 2 else right,
            )
        )
        halos[-1].start()
        locals_.append(
            pltpu.make_async_copy(own_kv.at[rows], window_ref.at[pl.ds(1024 + s * SEG, SEG)], local_sem.at[s])
        )
        locals_[-1].start()
    for s in range(4):
        for slot in range(4 * s, 4 * s + 4):

            @pl.when(slot != me)
            def _():
                remote(qg_in.at[slot], qg_in.at[slot], qg_ss.at[0], qg_rs.at[slot], left).wait_recv()

        rows = pl.ds(s * SEG, SEG)
        own_qg[rows, :] = jnp.dot(
            picks[s], qg_in[4 * s : 4 * s + 4].reshape(SEG, 128), preferred_element_type=jnp.float32
        ).astype(jnp.bfloat16)
        locals_.append(pltpu.make_async_copy(own_qg.at[rows], qg_ref.at[rows], local_sem.at[4 + s]))
        locals_[-1].start()
    for copy in halos:
        copy.wait()
    for copy in small + sends:
        copy.wait_send()
    for copy in locals_:
        copy.wait()


def attend_kernel(meta_ref, window_ref, qg_ref, aq_ref, own_ref, halo_ref, both, total):
    total[...] = jnp.zeros_like(total)
    low = lax.broadcasted_iota(jnp.int32, (BLK, 128), 1) < DIM

    def one_block(b, carry):
        seg, row = b // 4, b % 4
        live = meta_ref[seg, 4, row]
        steps = (live + 1) // 2
        rows = pl.ds(pl.multiple_of(b * BLK, BLK), BLK)
        qg = qg_ref[rows, :]
        zero = jnp.zeros_like(qg)
        pair = jnp.concatenate([jnp.where(low, qg, zero), jnp.where(low, zero, qg)], axis=0)

        def span(e):
            return pl.ds(pl.multiple_of((4 * seg + meta_ref[seg, row, e]) * BLK, BLK), BLK)

        def slot(e):
            return pl.ds(pl.multiple_of(e * BLK, BLK), BLK)

        def fold(x, op):
            return op(x.reshape(BLK // 8, 8, 128), axis=0)

        def scores(step, top):
            for u in range(2):
                e = 2 * step + u
                kv = window_ref[span(e), :]
                out = lax.dot_general(kv, pair, NT, preferred_element_type=jnp.float32)
                score = jnp.where(e < live, out[:, :BLK], -jnp.inf)
                both[slot(e), :BLK] = score
                both[slot(e), BLK:] = out[:, BLK:]
                top = jnp.maximum(top, fold(score, jnp.max))
            return top

        top = lax.fori_loop(0, steps, scores, jnp.full((8, 128), -jnp.inf, jnp.float32))
        top = jnp.max(top, axis=0, keepdims=True) * LOG2E

        def weigh(step, sums):
            mass, dot = sums
            for u in range(2):
                e = 2 * step + u
                part = jnp.exp2(both[slot(e), :BLK] * LOG2E - top)
                both[slot(e), :BLK] = part
                mass = mass + fold(part, jnp.sum)
                dot = dot + fold(part * both[slot(e), BLK:], jnp.sum)
            return mass, dot

        nought = jnp.zeros((8, 128), jnp.float32)
        mass, dot = lax.fori_loop(0, steps, weigh, (nought, nought))
        share = 1.0 / jnp.sum(mass, axis=0, keepdims=True)
        inner = jnp.sum(dot, axis=0, keepdims=True) * share

        def grads(step, acc):
            news = []
            for u in range(2):
                e = 2 * step + u
                chance = both[slot(e), :BLK] * share
                grad = chance * (both[slot(e), BLK:] - inner)
                w = jnp.concatenate([grad, chance], axis=1).astype(jnp.bfloat16)
                kv = window_ref[span(e), :]
                acc = acc + lax.dot_general(kv, w, TN, preferred_element_type=jnp.float32)
                news.append(total[span(e), :] + jnp.dot(w, pair, preferred_element_type=jnp.float32))
            for u in range(2):
                total[span(2 * step + u), :] = news[u]
            return acc

        acc = lax.fori_loop(0, steps, grads, jnp.zeros((128, 2 * BLK), jnp.float32))
        out = jnp.concatenate([acc[:DIM, :BLK] * SCALE, acc[DIM:, BLK:]], axis=0)
        aq_ref[rows, :] = jnp.transpose(out).astype(jnp.bfloat16)
        return carry

    lax.fori_loop(0, 16, one_block, 0)
    own_ref[...] = total[1024:3072, :]
    halo_ref[0:1024, :] = total[0:1024, :].astype(jnp.bfloat16)
    halo_ref[1024:2048, :] = total[3072:4096, :].astype(jnp.bfloat16)


def leave_kernel(
    aq_ref, own_ref, halo_ref, orders_ref,
    out_ref, dq_ref, dk_ref, dv_ref,
    aq_nat, kv_nat, halo_in, aq_in, kv_in,
    halo_ss, halo_rs, aq_ss, aq_rs, kv_ss, kv_rs,
):
    quad, me, left, right = place()
    greet(quad, me, left, right)
    half = pl.ds(0, 1024), pl.ds(1024, 1024)
    halos = [
        remote(halo_ref.at[half[0]], halo_in.at[half[1]], halo_ss.at[0], halo_rs.at[0], left),
        remote(halo_ref.at[half[1]], halo_in.at[half[0]], halo_ss.at[1], halo_rs.at[1], right),
    ]
    for copy in halos:
        copy.start()

    def one_hot(s):
        order = jnp.broadcast_to(orders_ref[s], (SEG, SEG))
        return (order == lax.broadcasted_iota(jnp.int32, (SEG, SEG), 0)).astype(jnp.bfloat16)

    def spread(nat, arrived, ssem, rsem, s):
        for part in range(4):
            slot = 4 * s + part
            copy = remote(
                nat.at[pl.ds(slot * BLK, BLK)], arrived.at[me], ssem.at[slot], rsem.at[me],
                member(quad, slot),
            )

            @pl.when(slot != me)
            def _():
                copy.start()

            @pl.when(slot == me)
            def _():
                arrived[me] = nat[pl.ds(slot * BLK, BLK), :]

    for s in range(4):
        rows = pl.ds(s * SEG, SEG)
        aq_nat[rows, :] = jnp.dot(
            one_hot(s), aq_ref[rows, :], preferred_element_type=jnp.float32
        ).astype(jnp.bfloat16)
        spread(aq_nat, aq_in, aq_ss, aq_rs, s)
    for h in (1, 0):
        halos[h].wait_recv()
        for s in (0, 1) if h == 1 else (2, 3):
            rows = pl.ds(s * SEG, SEG)
            whole = (own_ref[rows, :] + halo_in[rows, :].astype(jnp.float32)).astype(jnp.bfloat16)
            kv_nat[rows, :] = jnp.dot(
                one_hot(s), whole, preferred_element_type=jnp.float32
            ).astype(jnp.bfloat16)
            spread(kv_nat, kv_in, kv_ss, kv_rs, s)

    def collect(arrived, ssem, rsem, low_ref, high_ref):
        for slot in range(GROUP):

            @pl.when(slot != me)
            def _():
                remote(arrived.at[slot], arrived.at[slot], ssem.at[0], rsem.at[slot], left).wait_recv()

        for t in range(8):
            cols = slice(t * 128, t * 128 + 128)
            a, b = arrived[2 * t], arrived[2 * t + 1]
            low_ref[:, cols] = jnp.concatenate([a[:, :DIM], b[:, :DIM]], axis=1)
            high_ref[:, cols] = jnp.concatenate([a[:, DIM:], b[:, DIM:]], axis=1)

    collect(aq_in, aq_ss, aq_rs, dq_ref, out_ref)
    collect(kv_in, kv_ss, kv_rs, dk_ref, dv_ref)
    for copy in halos:
        copy.wait_send()
    for slot in range(GROUP):

        @pl.when(slot != me)
        def _():
            remote(aq_in.at[slot], aq_in.at[slot], aq_ss.at[slot], aq_rs.at[slot], left).wait_send()
            remote(kv_in.at[slot], kv_in.at[slot], kv_ss.at[slot], kv_rs.at[slot], left).wait_send()


def sems(*counts):
    return [pltpu.SemaphoreType.DMA((n,)) for n in counts]


def body(queries, keys, values, out_grad, node_order, block_lists, block_counts):
    bf, f32, i32 = jnp.bfloat16, jnp.float32, jnp.int32
    shape = jax.ShapeDtypeStruct
    slabs = pltpu.VMEM((GROUP, BLK, 128), bf)
    rows = pltpu.VMEM((4 * SEG, 128), bf)
    window, qg, orders, meta = pl.pallas_call(
        enter_kernel,
        out_shape=[
            shape((8 * SEG, 128), bf),
            shape((4 * SEG, 128), bf),
            shape((4, 1, SEG), i32),
            shape((4, 8, 128), i32),
        ],
        in_specs=[VMEM] * 7,
        out_specs=[ANY] * 4,
        scratch_shapes=[
            slabs, slabs, slabs, slabs, rows, rows,
            pltpu.VMEM((4, 1, SEG), i32), pltpu.VMEM((4, 8, 128), i32),
            *sems(16, 16, 16, 16, 4, 4, 4, 4, 4, 4, 10),
        ],
        compiler_params=pltpu.CompilerParams(
            collective_id=0, has_side_effects=True, vmem_limit_bytes=40 * 2**20
        ),
        name="enter",
    )(
        queries, keys, values, out_grad,
        node_order.reshape(1, SEG), block_lists, block_counts.reshape(1, 4),
    )
    aq, own, halo = pl.pallas_call(
        attend_kernel,
        out_shape=[shape((4 * SEG, 128), bf), shape((4 * SEG, 128), f32), shape((4 * SEG, 128), bf)],
        in_specs=[SMEM, VMEM, VMEM],
        out_specs=[VMEM] * 3,
        scratch_shapes=[pltpu.VMEM((LIST * BLK, 2 * BLK), f32), pltpu.VMEM((8 * SEG, 128), f32)],
        compiler_params=pltpu.CompilerParams(vmem_limit_bytes=40 * 2**20),
        name="attend",
    )(meta, window, qg)
    return pl.pallas_call(
        leave_kernel,
        out_shape=[shape((BLK, 16 * DIM), bf)] * 4,
        in_specs=[VMEM, VMEM, ANY, VMEM],
        out_specs=[VMEM] * 4,
        scratch_shapes=[
            rows, rows, rows, slabs, slabs,
            *sems(2, 2, 16, 16, 16, 16),
        ],
        compiler_params=pltpu.CompilerParams(
            collective_id=1, has_side_effects=True, vmem_limit_bytes=40 * 2**20
        ),
        name="leave",
    )(aq, own, halo, orders)


def solution(mesh):
    rows = P(("blk", "head"), None)
    return jax.shard_map(
        body,
        mesh=mesh,
        in_specs=(rows, rows, rows, rows, P("blk"), P("blk", None), P("blk")),
        out_specs=(rows, rows, rows, rows),
        check_vma=False,
    )
```

time: 384 us -> 92.1 us (0.24)
  the two profiles are of different devices: /device:TPU:102 before, /device:TPU:1 now
where the time goes in v1:
time: 92.1 us; the launch traced here: 91.9 us
  Pallas kernels  83.2 us (90%)
  local copies, waits for them, and re-layouts  7.96 us (9%)
    pallas_call x1, Pallas kernels, body(): pl.pallas_call(enter_kernel, out_shape=[shape((8 * SEG, 128), bf), shape(...  37.2 us
    pallas_call x1, Pallas kernels, body(): pl.pallas_call(leave_kernel, out_shape=[shape((BLK, 16 * DIM), bf)] * 4,...  27 us
    pallas_call x1, Pallas kernels, body(): pl.pallas_call(attend_kernel, out_shape=[shape((4 * SEG, 128), bf), shape...  18.9 us
    unnamed x18, local copies, waits for them, and re-layouts  7.96 us

profile of v1, /device:TPU:1, one launch (start us, length us, event | category | flops | bytes accessed | tf_op | source)
XLA Modules:
  0.0 91.9 jit_solution(12207671298844823866)
XLA Ops:
  0.6 0.0 copy-start.4
  0.6 0.0 copy-start.6
  0.7 0.7 copy-done.4
  1.3 0.0 copy-done.6
  1.3 0.0 copy-start
  1.3 0.9 %copy-done = bf16[128,1024]{1,0:T(8,128)(2,1)S(1)} copy-done((bf16[128,1024]{1,0:T(8,128)(2,1)S(1)}, bf16[128,1024]{1,0:T(8,128)(2,1)}, u32[]{:S(2)}) %copy-start) | copy-done | bytes 262168
  2.3 0.0 copy-start.1
  2.3 0.9 %copy-done.1 = bf16[128,1024]{1,0:T(8,128)(2,1)S(1)} copy-done((bf16[128,1024]{1,0:T(8,128)(2,1)S(1)}, bf16[128,1024]{1,0:T(8,128)(2,1)}, u32[]{:S(2)}) %copy-start.1) | copy-done | bytes 262168
  3.2 0.0 copy-start.2
  3.2 0.9 %copy-done.2 = bf16[128,1024]{1,0:T(8,128)(2,1)S(1)} copy-done((bf16[128,1024]{1,0:T(8,128)(2,1)S(1)}, bf16[128,1024]{1,0:T(8,128)(2,1)}, u32[]{:S(2)}) %copy-start.2) | copy-done | bytes 262168
  4.2 0.0 copy-start.3
  4.2 0.9 %copy-done.3 = bf16[128,1024]{1,0:T(8,128)(2,1)S(1)} copy-done((bf16[128,1024]{1,0:T(8,128)(2,1)S(1)}, bf16[128,1024]{1,0:T(8,128)(2,1)}, u32[]{:S(2)}) %copy-start.3) | copy-done | bytes 262168
  5.1 0.0 copy-start.5
  5.1 0.7 copy-done.5
  5.8 37.2 %enter.1 = (bf16[4096,128]{1,0:T(8,128)(2,1)S(1)}, bf16[2048,128]{1,0:T(8,128)(2,1)S(1)}, s32[4,1,512]{2,1,0:T(1,128)S(1)}, s32[4,8,128]{2,1,0:T(8,128)S(1)}) custom-call(bf16[128,1024]{1,0:T(8,128)(2,1)S(1)} %copy-done, bf16[128,1024]{1,0:T(8,128)(2,1)S(1)} %copy-done.1, bf16[128,1024]{1,0:T(8,128)(2,1)S(1)} %copy-done.2, bf16[128,1024]{1,0:T(8,128)(2,1)S(1)} %copy-done.3, ...), custom_call_target="tpu_custom_call" | custom-call | tf_op jit(solution)/shard_map/enter/pallas_call | solution.py:332
  43.0 18.9 %attend.1 = (bf16[2048,128]{1,0:T(8,128)(2,1)S(1)}, f32[2048,128]{1,0:T(8,128)S(1)}, bf16[2048,128]{1,0:T(8,128)(2,1)S(1)}) custom-call(s32[4,8,128]{2,1,0:T(8,128)S(1)} %get-tuple-element.11.meta_ref, bf16[4096,128]{1,0:T(8,128)(2,1)S(1)} %get-tuple-element.12.window_ref, bf16[2048,128]{1,0:T(8,128)(2,1)S(1)} %get-tuple-element.13.qg_ref), custom_call_target="tpu_custom_call" | custom-call | tf_op jit(solution)/shard_map/attend/pallas_call | solution.py:355
  62.0 27.0 %leave.1 = (bf16[128,1024]{1,0:T(8,128)(2,1)S(1)}, bf16[128,1024]{1,0:T(8,128)(2,1)S(1)}, bf16[128,1024]{1,0:T(8,128)(2,1)S(1)}, bf16[128,1024]{1,0:T(8,128)(2,1)S(1)}) custom-call(bf16[2048,128]{1,0:T(8,128)(2,1)S(1)} %get-tuple-element.14.aq_ref, f32[2048,128]{1,0:T(8,128)S(1)} %get-tuple-element.15.own_ref, ...), custom_call_target="tpu_custom_call" | custom-call | tf_op jit(solution)/shard_map/leave/pallas_call | solution.py:364
  89.0 0.7 copy.15
  89.7 0.7 copy.16
  90.4 0.7 copy.17
  91.1 0.7 copy.18
Async XLA Ops:
  0.6 0.7 copy-start.4
  0.6 0.7 copy-start.6
  1.3 1.0 %copy-start = (bf16[128,1024]{1,0:T(8,128)(2,1)S(1)}, bf16[128,1024]{1,0:T(8,128)(2,1)}, u32[]{:S(2)}) copy-start(bf16[128,1024]{1,0:T(8,128)(2,1)} %q_ref.1) | copy-start | bytes 786436
  2.3 0.9 %copy-start.1 = (bf16[128,1024]{1,0:T(8,128)(2,1)S(1)}, bf16[128,1024]{1,0:T(8,128)(2,1)}, u32[]{:S(2)}) copy-start(bf16[128,1024]{1,0:T(8,128)(2,1)} %k_ref.1) | copy-start | bytes 786436
  3.2 0.9 %copy-start.2 = (bf16[128,1024]{1,0:T(8,128)(2,1)S(1)}, bf16[128,1024]{1,0:T(8,128)(2,1)}, u32[]{:S(2)}) copy-start(bf16[128,1024]{1,0:T(8,128)(2,1)} %v_ref.1) | copy-start | bytes 786436
  4.2 0.9 %copy-start.3 = (bf16[128,1024]{1,0:T(8,128)(2,1)S(1)}, bf16[128,1024]{1,0:T(8,128)(2,1)}, u32[]{:S(2)}) copy-start(bf16[128,1024]{1,0:T(8,128)(2,1)} %g_ref.1) | copy-start | bytes 786436
  5.1 0.7 copy-start.5

commit v2 on v1

v2 whole, which is shorter than its diff:
```python
import functools
import math

import jax
import jax.numpy as jnp
from jax import lax
from jax.experimental import pallas as pl
from jax.experimental.pallas import tpu as pltpu
from jax.sharding import PartitionSpec as P

BLK = 128
SEG = 512
DIM = 64
LIST = 12
UNROLL = 8
GROUP = 16
NT = (((1,), (1,)), ((), ()))
TN = (((0,), (0,)), ((), ()))
SCALE = 1.0 / math.sqrt(DIM)
LOG2E = math.log2(math.e)
MESH = pl.DeviceIdType.MESH
HBM = pl.BlockSpec(memory_space=pltpu.HBM)
VMEM = pl.BlockSpec(memory_space=pltpu.VMEM)
SMEM = pl.BlockSpec(memory_space=pltpu.SMEM)


def flip(slot, half):
    return slot + half * (2 - 4 * (slot // 2 % 2))


def place():
    blk, head = lax.axis_index("blk"), lax.axis_index("head")
    quads = lax.axis_size("blk") // 4
    quad, part = blk // 4, (blk % 4) * 4 + head
    half = quad // (quads // 2)
    role = flip(part, half)
    sides = []
    for step in (quads - 1, 1):
        there = lax.rem(quad + step, quads)
        sides.append(member(there, flip(role, there // (quads // 2))))
    return quad, half, part, role, sides[0], sides[1]


def member(quad, part):
    return (quad * 4 + part // 4, part % 4)


OTHERS = [(x, 1, c) for x in (0, 1, 2, 3) for c in (0, 1)]
OTHERS += [(x, 0, c) for x in (2, 1, 3) for c in (0, 1)] + [(0, 0, 1)]


def other(part, steps):
    x, y, c = part // 4, part // 2 % 2, part % 2
    dx, dy, dc = steps
    x = lax.rem(x + dx, 4)
    y = 1 - y if dy else y
    c = 1 - c if dc else c
    return x * 4 + y * 2 + c


def remote(src, dst, ssem, rsem, device):
    return pltpu.make_async_remote_copy(
        src_ref=src, dst_ref=dst, send_sem=ssem, recv_sem=rsem, device_id=device, device_id_type=MESH
    )


def greet(quad, part, left, right):
    barrier = pltpu.get_barrier_semaphore()
    for steps in OTHERS:
        pl.semaphore_signal(
            barrier, inc=1, device_id=member(quad, other(part, steps)), device_id_type=MESH
        )
    for device in (left, right):
        pl.semaphore_signal(barrier, inc=1, device_id=device, device_id_type=MESH)


def await_greetings():
    pl.semaphore_wait(pltpu.get_barrier_semaphore(), GROUP + 1)


def enter_kernel(
    q_hbm, k_hbm, v_hbm, g_hbm, order_hbm, lists_hbm, counts_hbm,
    window_ref, qg_ref, orders_ref, meta_ref,
    q_ref, k_ref, v_ref, g_ref, lists_ref, counts_ref,
    kv_out, qg_out, kv_in, qg_in, own_kv, order_in, meta_in,
    kv_ss, kv_rs, qg_ss, qg_rs, order_ss, order_rs, meta_ss, meta_rs, halo_ss, halo_rs, local_sem,
):
    quad, half, part, role, left, right = place()
    seg = part // 4
    pulls = [
        pltpu.make_async_copy(src, dst, local_sem.at[i])
        for i, (src, dst) in enumerate(
            (
                (k_hbm, k_ref), (v_hbm, v_ref), (lists_hbm, lists_ref), (counts_hbm, counts_ref),
                (order_hbm, order_in.at[seg]), (q_hbm, q_ref), (g_hbm, g_ref),
            )
        )
    ]
    for copy in pulls:
        copy.start()
    greet(quad, part, left, right)
    for copy in pulls[:2]:
        copy.wait()
    for t in range(8):
        cols = slice(t * 128, t * 128 + 128)
        k, v = k_ref[:, cols], v_ref[:, cols]
        kv_out[2 * t] = jnp.concatenate([k[:, :DIM], v[:, :DIM]], axis=1)
        kv_out[2 * t + 1] = jnp.concatenate([k[:, DIM:], v[:, DIM:]], axis=1)
    await_greetings()
    sends = []
    for i, steps in enumerate(OTHERS):
        there = other(part, steps)
        sends.append(
            remote(
                kv_out.at[flip(there, half)], kv_in.at[part], kv_ss.at[i], kv_rs.at[part],
                member(quad, there),
            )
        )
        sends[-1].start()
    for copy in pulls[2:5]:
        copy.wait()
    meta_in[seg] = jnp.zeros((8, 128), jnp.int32)
    meta_in[seg, 0:4, 0:LIST] = lists_ref[...]
    meta_in[seg, 4:5, 0:4] = counts_ref[...]
    for step in range(1, 4):
        peer = member(quad, other(part, (step, 0, 0)))
        for ref, ssem, rsem in ((order_in, order_ss, order_rs), (meta_in, meta_ss, meta_rs)):
            sends.append(remote(ref.at[seg], ref.at[seg], ssem.at[step], rsem.at[seg], peer))
            sends[-1].start()
    kv_in[part] = kv_out[role]
    for copy in pulls[5:]:
        copy.wait()
    for t in range(8):
        cols = slice(t * 128, t * 128 + 128)
        q, g = q_ref[:, cols] * SCALE, g_ref[:, cols]
        qg_out[2 * t] = jnp.concatenate([q[:, :DIM], g[:, :DIM]], axis=1)
        qg_out[2 * t + 1] = jnp.concatenate([q[:, DIM:], g[:, DIM:]], axis=1)
    for i, steps in enumerate(OTHERS):
        there = other(part, steps)
        sends.append(
            remote(
                qg_out.at[flip(there, half)], qg_in.at[part], qg_ss.at[i], qg_rs.at[part],
                member(quad, there),
            )
        )
        sends[-1].start()
    qg_in[part] = qg_out[role]

    for s in range(4):

        @pl.when(s != seg)
        def _():
            remote(order_in.at[s], order_in.at[s], order_ss.at[0], order_rs.at[s], left).wait_recv()
            remote(meta_in.at[s], meta_in.at[s], meta_ss.at[0], meta_rs.at[s], left).wait_recv()

    def one_hot(s):
        order = jnp.broadcast_to(order_in[s].astype(jnp.float32), (128, SEG))
        order = jnp.transpose(order)
        lane = lax.broadcasted_iota(jnp.int32, (SEG, 128), 1).astype(jnp.float32)
        tiles = [(order == lane + 128.0 * t).astype(jnp.bfloat16) for t in range(4)]
        return jnp.concatenate(tiles, axis=1)

    picks = [one_hot(s) for s in range(4)]
    orders_ref[...] = order_in[...]
    meta_ref[...] = meta_in[...]
    halos, keeps = [], []
    for s in range(4):
        for slot in range(4 * s, 4 * s + 4):

            @pl.when(slot != part)
            def _():
                remote(kv_in.at[slot], kv_in.at[slot], kv_ss.at[0], kv_rs.at[slot], left).wait_recv()

        rows = pl.ds(s * SEG, SEG)
        own_kv[rows, :] = jnp.dot(
            picks[s], kv_in[4 * s : 4 * s + 4].reshape(SEG, 128), preferred_element_type=jnp.float32
        ).astype(jnp.bfloat16)
        there = 3072 + s * SEG if s < 2 else (s - 2) * SEG
        halos.append(
            remote(
                own_kv.at[rows], window_ref.at[pl.ds(there, SEG)], halo_ss.at[s], halo_rs.at[s],
                left if s < 2 else right,
            )
        )
        halos[-1].start()
        keeps.append(
            pltpu.make_async_copy(own_kv.at[rows], window_ref.at[pl.ds(1024 + s * SEG, SEG)], local_sem.at[s])
        )
        keeps[-1].start()
    for s in range(4):
        for slot in range(4 * s, 4 * s + 4):

            @pl.when(slot != part)
            def _():
                remote(qg_in.at[slot], qg_in.at[slot], qg_ss.at[0], qg_rs.at[slot], left).wait_recv()

        qg_ref[pl.ds(s * SEG, SEG), :] = jnp.dot(
            picks[s], qg_in[4 * s : 4 * s + 4].reshape(SEG, 128), preferred_element_type=jnp.float32
        ).astype(jnp.bfloat16)
    for copy in halos + keeps:
        copy.wait()
    for copy in sends:
        copy.wait_send()


def attend_kernel(
    meta_ref, window_ref, qg_ref, aq_ref, total_ref,
    block_of, span_of, pairs, turned, both, acc, top, mass, dot,
):
    low = lax.broadcasted_iota(jnp.int32, (BLK, 128), 1) < DIM
    live = 0
    for b in range(16):
        for e in range(LIST):
            block_of[live + e] = b
            span_of[live + e] = (b // 4 * 4 + meta_ref[b // 4, b % 4, e]) * BLK
        live = live + meta_ref[b // 4, 4, b % 4]
    for u in range(UNROLL):
        block_of[live + u] = 16
        span_of[live + u] = 0
    steps = (live + UNROLL - 1) // UNROLL
    for b in range(16):
        qg = qg_ref[b * BLK : b * BLK + BLK, :]
        zero = jnp.zeros_like(qg)
        pairs[b, :BLK] = jnp.where(low, qg, zero)
        pairs[b, BLK:] = jnp.where(low, zero, qg)
    pairs[16] = jnp.zeros((2 * BLK, 128), jnp.bfloat16)
    for w in range(32):
        rows = slice(w * BLK, w * BLK + BLK)
        turned[rows, :] = jnp.transpose(window_ref[rows, :])
    total_ref[...] = jnp.zeros_like(total_ref)
    acc[...] = jnp.zeros_like(acc)
    top[...] = jnp.full(top.shape, -jnp.inf, jnp.float32)
    mass[...] = jnp.zeros_like(mass)
    dot[...] = jnp.zeros_like(dot)

    def tile(step, u):
        t = step * UNROLL + u
        return t, block_of[t], pl.ds(pl.multiple_of(span_of[t], BLK), BLK)

    def lay(x):
        return x.reshape(BLK // 8, 8, 128)

    def scores(step, carry):
        for u in range(UNROLL):
            t, b, span = tile(step, u)
            out = lax.dot_general(window_ref[span, :], pairs[b], NT, preferred_element_type=jnp.float32)
            both[t] = out
            top[b] = jnp.maximum(top[b], jnp.max(lay(out[:, :BLK]), axis=0))
        return carry

    lax.fori_loop(0, steps, scores, 0)
    top[...] = jnp.broadcast_to(jnp.max(top[...], axis=1, keepdims=True) * LOG2E, top.shape)

    def weigh(step, carry):
        for u in range(UNROLL):
            t, b, _ = tile(step, u)
            part = jnp.exp2(lay(both[t, :, :BLK]) * LOG2E - top[b])
            both[t, :, :BLK] = part.reshape(BLK, BLK)
            mass[b] = mass[b] + jnp.sum(part, axis=0)
            dot[b] = dot[b] + jnp.sum(part * lay(both[t, :, BLK:]), axis=0)
        return carry

    lax.fori_loop(0, steps, weigh, 0)
    share = 1.0 / jnp.sum(mass[...], axis=1, keepdims=True)
    dot[...] = jnp.broadcast_to(jnp.sum(dot[...], axis=1, keepdims=True) * share, dot.shape)
    mass[...] = jnp.broadcast_to(share, mass.shape)

    def grads(step, carry):
        for u in range(UNROLL):
            t, b, span = tile(step, u)
            chance = lay(both[t, :, :BLK]) * mass[b]
            grad = chance * (lay(both[t, :, BLK:]) - dot[b])
            w = jnp.concatenate([grad.reshape(BLK, BLK), chance.reshape(BLK, BLK)], axis=1)
            w = w.astype(jnp.bfloat16)
            out = jnp.dot(turned[span, :], w, preferred_element_type=jnp.float32)
            acc[b, :DIM] = acc[b, :DIM] + out[:DIM, :BLK]
            acc[b, DIM:] = acc[b, DIM:] + out[DIM:, BLK:]
            total_ref[span, :] = total_ref[span, :] + jnp.dot(
                w, pairs[b], preferred_element_type=jnp.float32
            )
        return carry

    lax.fori_loop(0, steps, grads, 0)
    for b in range(16):
        out = jnp.concatenate([acc[b, :DIM] * SCALE, acc[b, DIM:]], axis=0).astype(jnp.bfloat16)
        aq_ref[b * BLK : b * BLK + BLK, :] = jnp.transpose(out)


def leave_kernel(
    aq_ref, total_ref, orders_ref,
    aq_in, kv_in,
    aq_nat, kv_nat, halo_out, halo_in,
    halo_ss, halo_rs, aq_ss, aq_rs, kv_ss, kv_rs,
):
    quad, half, part, role, left, right = place()
    greet(quad, part, left, right)
    halo_out[0:1024, :] = total_ref[0:1024, :].astype(jnp.bfloat16)
    halo_out[1024:2048, :] = total_ref[3072:4096, :].astype(jnp.bfloat16)

    def one_hot(s):
        order = jnp.broadcast_to(orders_ref[s], (SEG, SEG))
        return (order == lax.broadcasted_iota(jnp.int32, (SEG, SEG), 0)).astype(jnp.bfloat16)

    def put(nat, rows, x, pick):
        nat[rows, :] = jnp.dot(pick, x, preferred_element_type=jnp.float32).astype(jnp.bfloat16)

    picks = [one_hot(s) for s in range(4)]
    await_greetings()
    halos = []
    for i in (0, 2, 1, 3):
        here, there = pl.ds(i * SEG, SEG), pl.ds((i + 2) % 4 * SEG, SEG)
        halos.append(
            remote(
                halo_out.at[here], halo_in.at[there], halo_ss.at[i], halo_rs.at[(i + 2) % 4],
                left if i < 2 else right,
            )
        )
        halos[-1].start()

    def spread(nat, arrived, ssem, rsem, s):
        for slot in range(4 * s, 4 * s + 4):

            @pl.when(slot != part)
            def _():
                remote(
                    nat.at[pl.ds(slot * BLK, BLK)], arrived.at[role], ssem.at[slot], rsem.at[role],
                    member(quad, slot),
                ).start()

            @pl.when(slot == part)
            def _():
                arrived[role] = nat[pl.ds(slot * BLK, BLK), :]

    for s in range(4):
        rows = pl.ds(s * SEG, SEG)
        put(aq_nat, rows, aq_ref[rows, :], picks[s])
        spread(aq_nat, aq_in, aq_ss, aq_rs, s)
    for s in (2, 0, 3, 1):
        rows = pl.ds(s * SEG, SEG)
        remote(halo_in.at[rows], halo_in.at[rows], halo_ss.at[s], halo_rs.at[s], left).wait_recv()
        whole = total_ref[pl.ds(1024 + s * SEG, SEG), :] + halo_in[rows, :].astype(jnp.float32)
        put(kv_nat, rows, whole.astype(jnp.bfloat16), picks[s])
        spread(kv_nat, kv_in, kv_ss, kv_rs, s)
    for copy in halos:
        copy.wait_send()
    for slot in range(GROUP):

        @pl.when(slot != part)
        def _():
            for arrived, ssem, rsem in ((aq_in, aq_ss, aq_rs), (kv_in, kv_ss, kv_rs)):
                there = arrived.at[slot]
                remote(there, there, ssem.at[slot], rsem.at[slot], left).wait_send()

        @pl.when(slot != role)
        def _():
            for arrived, ssem, rsem in ((aq_in, aq_ss, aq_rs), (kv_in, kv_ss, kv_rs)):
                there = arrived.at[slot]
                remote(there, there, ssem.at[slot], rsem.at[slot], left).wait_recv()


def finish_kernel(aq_ref, kv_ref, out_ref, dq_ref, dk_ref, dv_ref):
    for arrived, low_ref, high_ref in ((aq_ref, dq_ref, out_ref), (kv_ref, dk_ref, dv_ref)):
        for t in range(8):
            cols = slice(t * 128, t * 128 + 128)
            a, b = arrived[2 * t], arrived[2 * t + 1]
            low_ref[:, cols] = jnp.concatenate([a[:, :DIM], b[:, :DIM]], axis=1)
            high_ref[:, cols] = jnp.concatenate([a[:, DIM:], b[:, DIM:]], axis=1)


def sems(*counts):
    return [pltpu.SemaphoreType.DMA((n,)) for n in counts]


def body(queries, keys, values, out_grad, node_order, block_lists, block_counts):
    bf, f32, i32 = jnp.bfloat16, jnp.float32, jnp.int32
    shape = jax.ShapeDtypeStruct
    slabs = pltpu.VMEM((GROUP, BLK, 128), bf)
    rows = pltpu.VMEM((4 * SEG, 128), bf)
    mine = pltpu.VMEM((BLK, 16 * DIM), bf)
    window, qg, orders, meta = pl.pallas_call(
        enter_kernel,
        out_shape=[
            shape((8 * SEG, 128), bf),
            shape((4 * SEG, 128), bf),
            shape((4, 1, SEG), i32),
            shape((4, 8, 128), i32),
        ],
        in_specs=[HBM] * 7,
        out_specs=[VMEM] * 4,
        scratch_shapes=[
            mine, mine, mine, mine, pltpu.VMEM((4, LIST), i32), pltpu.VMEM((1, 4), i32),
            slabs, slabs, slabs, slabs, rows,
            pltpu.VMEM((4, 1, SEG), i32), pltpu.VMEM((4, 8, 128), i32),
            *sems(16, 16, 16, 16, 4, 4, 4, 4, 4, 4, 7),
        ],
        compiler_params=pltpu.CompilerParams(
            collective_id=0, has_side_effects=True, vmem_limit_bytes=16 * 2**20
        ),
        name="enter",
    )(
        *(
            pltpu.with_memory_space_constraint(x, pltpu.HBM)
            for x in (
                queries, keys, values, out_grad,
                node_order.reshape(1, SEG), block_lists, block_counts.reshape(1, 4),
            )
        )
    )
    stats = pltpu.VMEM((17, 8, 128), f32)
    aq, total = pl.pallas_call(
        attend_kernel,
        out_shape=[shape((4 * SEG, 128), bf), shape((8 * SEG, 128), f32)],
        in_specs=[SMEM, VMEM, VMEM],
        out_specs=[VMEM] * 2,
        scratch_shapes=[
            pltpu.SMEM((16 * LIST + 16,), i32), pltpu.SMEM((16 * LIST + 16,), i32),
            pltpu.VMEM((17, 2 * BLK, 128), bf), pltpu.VMEM((8 * SEG, 128), bf),
            pltpu.VMEM((16 * LIST + 8, BLK, 2 * BLK), f32), pltpu.VMEM((17, 128, BLK), f32),
            stats, stats, stats,
        ],
        compiler_params=pltpu.CompilerParams(vmem_limit_bytes=40 * 2**20),
        name="attend",
    )(meta, window, qg)
    aq_in, kv_in = pl.pallas_call(
        leave_kernel,
        out_shape=[shape((GROUP, BLK, 128), bf)] * 2,
        in_specs=[VMEM] * 3,
        out_specs=[VMEM] * 2,
        scratch_shapes=[rows, rows, rows, rows, *sems(4, 4, 16, 16, 16, 16)],
        compiler_params=pltpu.CompilerParams(
            collective_id=1, has_side_effects=True, vmem_limit_bytes=16 * 2**20
        ),
        name="leave",
    )(aq, total, orders)
    return pl.pallas_call(
        finish_kernel,
        out_shape=[shape((BLK, 16 * DIM), bf)] * 4,
        in_specs=[VMEM] * 2,
        out_specs=[VMEM] * 4,
        compiler_params=pltpu.CompilerParams(vmem_limit_bytes=8 * 2**20),
        name="finish",
    )(aq_in, kv_in)


def solution(mesh):
    rows = P(("blk", "head"), None)
    return jax.shard_map(
        body,
        mesh=mesh,
        in_specs=(rows, rows, rows, rows, P("blk"), P("blk", None), P("blk")),
        out_specs=(rows, rows, rows, rows),
        check_vma=False,
    )
```

time: 92.1 us -> 61.5 us (0.67)
  the two profiles are of different devices: /device:TPU:1 before, /device:TPU:27 now
where the time goes in v2:
time: 61.5 us; the launch traced here: 61.4 us
  Pallas kernels  60.8 us (99%)
  between operations  0.66 us (1%)
    pallas_call x1, Pallas kernels, body(): pl.pallas_call(enter_kernel, out_shape=[shape((8 * SEG, 128), bf), shape(...  25.8 us
    pallas_call x1, Pallas kernels, body(): pl.pallas_call(leave_kernel, out_shape=[shape((GROUP, BLK, 128), bf)] * 2...  22.3 us
    pallas_call x1, Pallas kernels, body(): pl.pallas_call(attend_kernel, out_shape=[shape((4 * SEG, 128), bf), shape...  11.3 us
    pallas_call x1, Pallas kernels, body(): pl.pallas_call(finish_kernel, out_shape=[shape((BLK, 16 * DIM), bf)] * 4,...  1.26 us

profile of v2, /device:TPU:27, one launch (start us, length us, event | category | flops | bytes accessed | tf_op | source)
XLA Modules:
  0.0 61.4 jit_solution(6833186615331809223)
XLA Ops:
  0.6 25.8 %enter.1 = (bf16[4096,128]{1,0:T(8,128)(2,1)S(1)}, bf16[2048,128]{1,0:T(8,128)(2,1)S(1)}, s32[4,1,512]{2,1,0:T(1,128)S(1)}, s32[4,8,128]{2,1,0:T(8,128)S(1)}) custom-call(bf16[128,1024]{1,0:T(8,128)(2,1)} %q_hbm.1, bf16[128,1024]{1,0:T(8,128)(2,1)} %k_hbm.1, bf16[128,1024]{1,0:T(8,128)(2,1)} %v_hbm.1, bf16[128,1024]{1,0:T(8,128)(2,1)} %g_hbm.1, ...), custom_call_target="tpu_custom_call" | custom-call | tf_op jit(solution)/shard_map/enter/pallas_call | solution.py:380
  26.5 11.3 %attend.1 = (bf16[2048,128]{1,0:T(8,128)(2,1)S(1)}, f32[4096,128]{1,0:T(8,128)S(1)}) custom-call(s32[4,8,128]{2,1,0:T(8,128)S(1)} %get-tuple-element.12.meta_ref, bf16[4096,128]{1,0:T(8,128)(2,1)S(1)} %get-tuple-element.13.window_ref, bf16[2048,128]{1,0:T(8,128)(2,1)S(1)} %get-tuple-element.14.qg_ref), custom_call_target="tpu_custom_call" | custom-call | tf_op jit(solution)/shard_map/attend/pallas_call | solution.py:410
  37.8 22.3 %leave.1 = (bf16[16,128,128]{2,1,0:T(8,128)(2,1)S(1)}, bf16[16,128,128]{2,1,0:T(8,128)(2,1)S(1)}) custom-call(bf16[2048,128]{1,0:T(8,128)(2,1)S(1)} %get-tuple-element.15.aq_ref, f32[4096,128]{1,0:T(8,128)S(1)} %get-tuple-element.16.total_ref, s32[4,1,512]{2,1,0:T(1,128)S(1)} %get-tuple-element.17.orders_ref), custom_call_target="tpu_custom_call" | custom-call | tf_op jit(solution)/shard_map/leave/pallas_call | solution.py:424
  60.2 1.3 %finish.1 = (bf16[128,1024]{1,0:T(8,128)(2,1)}, bf16[128,1024]{1,0:T(8,128)(2,1)}, bf16[128,1024]{1,0:T(8,128)(2,1)}, bf16[128,1024]{1,0:T(8,128)(2,1)}) custom-call(bf16[16,128,128]{2,1,0:T(8,128)(2,1)S(1)} %get-tuple-element.18.aq_ref, bf16[16,128,128]{2,1,0:T(8,128)(2,1)S(1)} %get-tuple-element.19.kv_ref), custom_call_target="tpu_custom_call" | custom-call | tf_op jit(solution)/shard_map/finish/pallas_call | solution.py:435

commit v3 on v2

v3 whole, which is shorter than its diff:
```python
import functools
import math

import jax
import jax.numpy as jnp
from jax import lax
from jax.experimental import pallas as pl
from jax.experimental.pallas import tpu as pltpu
from jax.sharding import PartitionSpec as P

BLK = 128
SEG = 512
DIM = 64
LIST = 12
UNROLL = 16
GROUP = 16
NT = (((1,), (1,)), ((), ()))
TN = (((0,), (0,)), ((), ()))
SCALE = 1.0 / math.sqrt(DIM)
LOG2E = math.log2(math.e)
MESH = pl.DeviceIdType.MESH
HBM = pl.BlockSpec(memory_space=pltpu.HBM)
VMEM = pl.BlockSpec(memory_space=pltpu.VMEM)
SMEM = pl.BlockSpec(memory_space=pltpu.SMEM)


def flip(slot, half):
    return slot + half * (2 - 4 * (slot // 2 % 2))


def place():
    blk, head = lax.axis_index("blk"), lax.axis_index("head")
    quads = lax.axis_size("blk") // 4
    quad, part = blk // 4, (blk % 4) * 4 + head
    half = quad // (quads // 2)
    role = flip(part, half)
    sides = []
    for step in (quads - 1, 1):
        there = lax.rem(quad + step, quads)
        sides.append(member(there, flip(role, there // (quads // 2))))
    return quad, half, part, role, sides[0], sides[1]


def member(quad, part):
    return (quad * 4 + part // 4, part % 4)


OTHERS = [
    (2, 1, 0), (2, 0, 0), (1, 1, 0), (3, 1, 0), (2, 1, 1), (2, 0, 1), (1, 0, 0), (3, 0, 0),
    (0, 1, 0), (1, 1, 1), (3, 1, 1), (0, 1, 1), (1, 0, 1), (3, 0, 1), (0, 0, 1),
]


def other(part, steps):
    x, y, c = part // 4, part // 2 % 2, part % 2
    dx, dy, dc = steps
    x = lax.rem(x + dx, 4)
    y = 1 - y if dy else y
    c = 1 - c if dc else c
    return x * 4 + y * 2 + c


def remote(src, dst, ssem, rsem, device):
    return pltpu.make_async_remote_copy(
        src_ref=src, dst_ref=dst, send_sem=ssem, recv_sem=rsem, device_id=device, device_id_type=MESH
    )


def greet(quad, part, left, right):
    barrier = pltpu.get_barrier_semaphore()
    for steps in OTHERS:
        pl.semaphore_signal(
            barrier, inc=1, device_id=member(quad, other(part, steps)), device_id_type=MESH
        )
    for device in (left, right):
        pl.semaphore_signal(barrier, inc=1, device_id=device, device_id_type=MESH)


def await_greetings():
    pl.semaphore_wait(pltpu.get_barrier_semaphore(), GROUP + 1)


def enter_kernel(
    q_hbm, k_hbm, v_hbm, g_hbm, order_hbm, lists_hbm, counts_hbm,
    window_ref, turned_ref, pairs_ref, meta_ref,
    q_ref, k_ref, v_ref, g_ref, order_ref, lists_ref, counts_ref,
    kv_out, qg_out, kv_in, qg_in, halo_in, meta_in, meta_halo, picks,
    kv_ss, kv_rs, qg_ss, qg_rs, halo_ss, halo_rs, meta_ss, meta_rs, side_ss, side_rs, local_sem,
):
    quad, half, part, role, left, right = place()
    seg = part // 4
    pulls = [
        pltpu.make_async_copy(src, dst, local_sem.at[i])
        for i, (src, dst) in enumerate(
            (
                (order_hbm, order_ref), (lists_hbm, lists_ref), (counts_hbm, counts_ref),
                (k_hbm, k_ref), (v_hbm, v_ref), (q_hbm, q_ref), (g_hbm, g_ref),
            )
        )
    ]
    for copy in pulls:
        copy.start()
    greet(quad, part, left, right)
    for copy in pulls[:3]:
        copy.wait()
    meta_in[seg] = jnp.zeros((16, 128), jnp.int32)
    for t in range(4):
        meta_in[seg, t : t + 1, :] = order_ref[:, t * 128 : t * 128 + 128]
    meta_in[seg, 4:8, 0:LIST] = lists_ref[...]
    meta_in[seg, 8:9, 0:4] = counts_ref[...]
    for copy in pulls[3:5]:
        copy.wait()
    for t in range(8):
        cols = slice(t * 128, t * 128 + 128)
        k, v = k_ref[:, cols], v_ref[:, cols]
        kv_out[2 * t] = jnp.concatenate([k[:, :DIM], v[:, :DIM]], axis=1)
        kv_out[2 * t + 1] = jnp.concatenate([k[:, DIM:], v[:, DIM:]], axis=1)
    await_greetings()
    sends = []

    def send(src, dst, ssem, rsem, device):
        sends.append(remote(src, dst, ssem, rsem, device))
        sends[-1].start()

    def scatter(i, out, arrived, ssem, rsem):
        there = other(part, OTHERS[i])
        send(out.at[flip(there, half)], arrived.at[part], ssem.at[i], rsem.at[part], member(quad, there))

    def landed(ref, rsem, slot):
        remote(ref.at[slot], ref.at[slot], kv_ss.at[0], rsem.at[slot], left).wait_recv()

    def pass_on(slot):
        device = [jnp.where(slot < 8, a, b) for a, b in zip(left, right)]
        there = lax.rem(slot + 8, GROUP)
        remote(kv_in.at[slot], halo_in.at[there], halo_ss.at[slot], halo_rs.at[there], device).start()

    for step in range(1, 4):
        peer = member(quad, other(part, (step, 0, 0)))
        send(meta_in.at[seg], meta_in.at[seg], meta_ss.at[step], meta_rs.at[seg], peer)
    for i in range(len(OTHERS)):
        scatter(i, kv_out, kv_in, kv_ss, kv_rs)
    kv_in[part] = kv_out[role]
    pass_on(part)
    for copy in pulls[5:]:
        copy.wait()
    for t in range(8):
        cols = slice(t * 128, t * 128 + 128)
        q, g = q_ref[:, cols] * SCALE, g_ref[:, cols]
        qg_out[2 * t] = jnp.concatenate([q[:, :DIM], g[:, :DIM]], axis=1)
        qg_out[2 * t + 1] = jnp.concatenate([q[:, DIM:], g[:, DIM:]], axis=1)
    for i in range(len(OTHERS)):
        scatter(i, qg_out, qg_in, qg_ss, qg_rs)
    qg_in[part] = qg_out[role]
    for step in range(1, 4):
        landed(meta_in, meta_rs, lax.rem(seg + step, 4))

    send(meta_in.at[0:2], meta_halo.at[2:4], side_ss.at[0], side_rs.at[1], left)
    send(meta_in.at[2:4], meta_halo.at[0:2], side_ss.at[1], side_rs.at[0], right)
    lane = lax.broadcasted_iota(jnp.int32, (SEG, 128), 1).astype(jnp.float32)

    def one_hot(at, meta):
        rows = meta[0:4].astype(jnp.float32)
        order = jnp.concatenate(
            [jnp.transpose(jnp.broadcast_to(rows[t : t + 1], (128, 128))) for t in range(4)], axis=0
        )
        for t in range(4):
            picks[at, :, t * 128 : t * 128 + 128] = (order == lane + 128.0 * t).astype(jnp.bfloat16)

    meta_ref[...] = meta_in[...]
    for dx, dy, dc in OTHERS:
        slot = other(part, (-dx % 4, dy, dc))
        landed(kv_in, kv_rs, slot)
        pass_on(slot)

    def blocked(pick, arrived, s):
        rows = arrived[4 * s : 4 * s + 4].reshape(SEG, 128)
        return jnp.dot(picks[pick], rows, preferred_element_type=jnp.float32).astype(jnp.bfloat16)

    def keep(at, kv):
        window_ref[at : at + SEG, :] = kv
        for i in range(0, SEG, BLK):
            turned_ref[at + i : at + i + BLK, :] = jnp.transpose(kv[i : i + BLK])

    for s in range(4):
        one_hot(s, meta_in[s])
    for side in range(2):
        two = meta_halo.at[2 * side : 2 * side + 2]
        remote(two, two, side_ss.at[side], side_rs.at[side], left).wait_recv()
        for s in (2 * side, 2 * side + 1):
            one_hot(4 + s, meta_halo[s])
    for s in range(4):
        keep(1024 + s * SEG, blocked(s, kv_in, s))
    for dx, dy, dc in OTHERS:
        landed(qg_in, qg_rs, other(part, (-dx % 4, dy, dc)))
    for slot in range(GROUP):
        landed(halo_in, halo_rs, slot)
    low = lax.broadcasted_iota(jnp.int32, (SEG, 128), 1) < DIM
    for s in range(4):
        qg = blocked(s, qg_in, s)
        zero = jnp.zeros_like(qg)
        pairs_ref[4 * s : 4 * s + 4, :BLK] = jnp.where(low, qg, zero).reshape(4, BLK, 128)
        pairs_ref[4 * s : 4 * s + 4, BLK:] = jnp.where(low, zero, qg).reshape(4, BLK, 128)
        keep((s if s < 2 else s + 4) * SEG, blocked(4 + s, halo_in, s))
    pairs_ref[16] = jnp.zeros((2 * BLK, 128), jnp.bfloat16)
    for copy in sends:
        copy.wait_send()
    for slot in range(GROUP):
        remote(kv_in.at[slot], kv_in.at[slot], halo_ss.at[slot], halo_rs.at[slot], left).wait_send()


def attend_kernel(
    meta_ref, window_ref, turned_ref, pairs, aq_ref, total_ref,
    block_of, first_of, second_of, whole_of, both, acc, top, mass, dot,
):
    live = 0
    for b in range(16):
        count = meta_ref[b // 4, 8, b % 4]
        for i in range(LIST // 2):
            block_of[live + i] = b
            first_of[live + i] = (b // 4 * 4 + meta_ref[b // 4, 4 + b % 4, 2 * i]) * BLK
            second_of[live + i] = (b // 4 * 4 + meta_ref[b // 4, 4 + b % 4, 2 * i + 1]) * BLK
            whole_of[live + i] = count - 2 * i - 1
        live = live + (count + 1) // 2
    for u in range(UNROLL):
        block_of[live + u] = 16
        first_of[live + u] = 0
        second_of[live + u] = BLK
        whole_of[live + u] = 0
    steps = (live + UNROLL - 1) // UNROLL
    total_ref[...] = jnp.zeros_like(total_ref)
    acc[...] = jnp.zeros_like(acc)
    top[...] = jnp.full(top.shape, -jnp.inf, jnp.float32)
    mass[...] = jnp.zeros_like(mass)
    dot[...] = jnp.zeros_like(dot)

    def tiles(step, u):
        t = step * UNROLL + u
        spans = [pl.ds(pl.multiple_of(ref[t], BLK), BLK) for ref in (first_of, second_of)]
        return t, block_of[t], spans[0], spans[1], whole_of[t] > 0

    def lay(x):
        return x.reshape(BLK // 8, 8, 128)

    def scores(step, carry):
        for u in range(UNROLL):
            t, b, one, two, whole = tiles(step, u)
            kv = jnp.concatenate([window_ref[one, :], window_ref[two, :]], axis=0)
            out = lax.dot_general(kv, pairs[b], NT, preferred_element_type=jnp.float32)
            both[t] = out
            high = jnp.max(lay(out[:BLK, :BLK]), axis=0)
            other_high = jnp.max(lay(out[BLK:, :BLK]), axis=0)
            high = jnp.maximum(high, jnp.where(whole, other_high, -jnp.inf))
            top[b] = jnp.maximum(top[b], high)
        return carry

    lax.fori_loop(0, steps, scores, 0)
    top[...] = jnp.broadcast_to(jnp.max(top[...], axis=1, keepdims=True) * LOG2E, top.shape)

    def weigh(step, carry):
        for u in range(UNROLL):
            t, b, _, _, whole = tiles(step, u)
            high = top[b]
            one = jnp.exp2(lay(both[t, :BLK, :BLK]) * LOG2E - high)
            two = jnp.exp2(lay(both[t, BLK:, :BLK]) * LOG2E - jnp.where(whole, high, jnp.inf))
            both[t, :BLK, :BLK] = one.reshape(BLK, BLK)
            both[t, BLK:, :BLK] = two.reshape(BLK, BLK)
            mass[b] = mass[b] + jnp.sum(one + two, axis=0)
            dot[b] = dot[b] + jnp.sum(
                one * lay(both[t, :BLK, BLK:]) + two * lay(both[t, BLK:, BLK:]), axis=0
            )
        return carry

    lax.fori_loop(0, steps, weigh, 0)
    share = 1.0 / jnp.sum(mass[...], axis=1, keepdims=True)
    dot[...] = jnp.broadcast_to(jnp.sum(dot[...], axis=1, keepdims=True) * share, dot.shape)
    mass[...] = jnp.broadcast_to(share, mass.shape)

    def grads(step, carry):
        for u in range(UNROLL):
            t, b, one, two, _ = tiles(step, u)
            chance = both[t, :, :BLK].reshape(BLK // 4, 8, 128) * mass[b]
            grad = chance * (both[t, :, BLK:].reshape(BLK // 4, 8, 128) - dot[b])
            w = jnp.concatenate([grad.reshape(2 * BLK, BLK), chance.reshape(2 * BLK, BLK)], axis=1)
            w = w.astype(jnp.bfloat16)
            kv = jnp.concatenate([turned_ref[one, :], turned_ref[two, :]], axis=1)
            out = jnp.dot(kv, w, preferred_element_type=jnp.float32)
            acc[b, :DIM] = acc[b, :DIM] + out[:DIM, :BLK]
            acc[b, DIM:] = acc[b, DIM:] + out[DIM:, BLK:]
            out = jnp.dot(w, pairs[b], preferred_element_type=jnp.float32)
            one_sum, two_sum = total_ref[one, :] + out[:BLK], total_ref[two, :] + out[BLK:]
            total_ref[one, :] = one_sum
            total_ref[two, :] = two_sum
        return carry

    lax.fori_loop(0, steps, grads, 0)
    for b in range(16):
        out = jnp.concatenate([acc[b, :DIM] * SCALE, acc[b, DIM:]], axis=0).astype(jnp.bfloat16)
        aq_ref[b * BLK : b * BLK + BLK, :] = jnp.transpose(out)


def leave_kernel(
    aq_ref, total_ref, meta_ref,
    aq_in, kv_in,
    aq_nat, kv_nat, halo_out, halo_in, picks,
    halo_ss, halo_rs, aq_ss, aq_rs, kv_ss, kv_rs,
):
    quad, half, part, role, left, right = place()
    greet(quad, part, left, right)
    halo_out[0:8] = total_ref[0:1024, :].astype(jnp.bfloat16).reshape(8, BLK, 128)
    halo_out[8:16] = total_ref[3072:4096, :].astype(jnp.bfloat16).reshape(8, BLK, 128)

    def natural(nat, s, x):
        x = jnp.dot(picks[s], x, preferred_element_type=jnp.float32).astype(jnp.bfloat16)
        nat[pl.ds(4 * s, 4)] = x.reshape(4, BLK, 128)

    for s in range(4):
        order = jnp.concatenate([meta_ref[s, t : t + 1, :] for t in range(4)], axis=1)
        here = lax.broadcasted_iota(jnp.int32, (SEG, SEG), 0)
        picks[s] = (jnp.broadcast_to(order, (SEG, SEG)) == here).astype(jnp.bfloat16)
        natural(aq_nat, s, aq_ref[s * SEG : s * SEG + SEG, :])
    await_greetings()
    turn = [lax.rem(part // 4 + d, 4) for d in (2, 1, 3, 0)]
    for i in range(GROUP):
        there = 4 * turn[i // 4] + i % 4
        here = lax.rem(there + 8, GROUP)
        device = [jnp.where(here < 8, a, b) for a, b in zip(left, right)]
        remote(halo_out.at[here], halo_in.at[there], halo_ss.at[here], halo_rs.at[there], device).start()
        if i < len(OTHERS):
            slot = other(part, OTHERS[i])
            remote(
                aq_nat.at[slot], aq_in.at[role], aq_ss.at[slot], aq_rs.at[role], member(quad, slot)
            ).start()
    aq_in[role] = aq_nat[part]
    for s, dx in zip(turn, (2, 1, 3, 0)):
        for p in range(4):
            piece = halo_in.at[4 * s + p]
            remote(piece, piece, halo_ss.at[0], halo_rs.at[4 * s + p], left).wait_recv()
        arrived = halo_in[pl.ds(4 * s, 4)].reshape(SEG, 128).astype(jnp.float32)
        whole = total_ref[pl.ds(pl.multiple_of(1024 + s * SEG, SEG), SEG), :] + arrived
        natural(kv_nat, s, whole.astype(jnp.bfloat16))
        for dy, dc in ((1, 0), (0, 1), (1, 1), (0, 0)):
            if (dx, dy, dc) != (0, 0, 0):
                slot = other(part, (dx, dy, dc))
                remote(
                    kv_nat.at[slot], kv_in.at[role], kv_ss.at[slot], kv_rs.at[role], member(quad, slot)
                ).start()
    kv_in[role] = kv_nat[part]
    for slot in range(GROUP):
        remote(halo_out.at[slot], halo_out.at[slot], halo_ss.at[slot], halo_rs.at[0], left).wait_send()

        @pl.when(slot != part)
        def _():
            for arrived, ssem, rsem in ((aq_in, aq_ss, aq_rs), (kv_in, kv_ss, kv_rs)):
                there = arrived.at[slot]
                remote(there, there, ssem.at[slot], rsem.at[slot], left).wait_send()

        @pl.when(slot != role)
        def _():
            for arrived, ssem, rsem in ((aq_in, aq_ss, aq_rs), (kv_in, kv_ss, kv_rs)):
                there = arrived.at[slot]
                remote(there, there, ssem.at[slot], rsem.at[slot], left).wait_recv()


def finish_kernel(aq_ref, kv_ref, out_ref, dq_ref, dk_ref, dv_ref):
    for arrived, low_ref, high_ref in ((aq_ref, dq_ref, out_ref), (kv_ref, dk_ref, dv_ref)):
        for t in range(8):
            cols = slice(t * 128, t * 128 + 128)
            a, b = arrived[2 * t], arrived[2 * t + 1]
            low_ref[:, cols] = jnp.concatenate([a[:, :DIM], b[:, :DIM]], axis=1)
            high_ref[:, cols] = jnp.concatenate([a[:, DIM:], b[:, DIM:]], axis=1)


def sems(*counts):
    return [pltpu.SemaphoreType.DMA((n,)) for n in counts]


def body(queries, keys, values, out_grad, node_order, block_lists, block_counts):
    bf, f32, i32 = jnp.bfloat16, jnp.float32, jnp.int32
    shape = jax.ShapeDtypeStruct
    slabs = pltpu.VMEM((GROUP, BLK, 128), bf)
    numbers = pltpu.VMEM((4, 16, 128), i32)
    mine = pltpu.VMEM((BLK, 16 * DIM), bf)
    window, turned, pairs, meta = pl.pallas_call(
        enter_kernel,
        out_shape=[
            shape((8 * SEG, 128), bf),
            shape((8 * SEG, 128), bf),
            shape((17, 2 * BLK, 128), bf),
            shape((4, 16, 128), i32),
        ],
        in_specs=[HBM] * 7,
        out_specs=[VMEM] * 4,
        scratch_shapes=[
            mine, mine, mine, mine,
            pltpu.VMEM((1, SEG), i32), pltpu.VMEM((4, LIST), i32), pltpu.VMEM((1, 4), i32),
            slabs, slabs, slabs, slabs, slabs, numbers, numbers, pltpu.VMEM((8, SEG, SEG), bf),
            *sems(16, 16, 16, 16, 16, 16, 4, 4, 2, 2, 7),
        ],
        compiler_params=pltpu.CompilerParams(
            collective_id=0, has_side_effects=True, vmem_limit_bytes=16 * 2**20
        ),
        name="enter",
    )(
        *(
            pltpu.with_memory_space_constraint(x, pltpu.HBM)
            for x in (
                queries, keys, values, out_grad,
                node_order.reshape(1, SEG), block_lists, block_counts.reshape(1, 4),
            )
        )
    )
    stats = pltpu.VMEM((17, 8, 128), f32)
    pairs_most = 8 * LIST + 16
    table = pltpu.SMEM((pairs_most,), i32)
    aq, total = pl.pallas_call(
        attend_kernel,
        out_shape=[shape((4 * SEG, 128), bf), shape((8 * SEG, 128), f32)],
        in_specs=[SMEM, VMEM, VMEM, VMEM],
        out_specs=[VMEM] * 2,
        scratch_shapes=[
            table, table, table, table,
            pltpu.VMEM((pairs_most, 2 * BLK, 2 * BLK), f32), pltpu.VMEM((17, 128, BLK), f32),
            stats, stats, stats,
        ],
        compiler_params=pltpu.CompilerParams(vmem_limit_bytes=40 * 2**20),
        name="attend",
    )(meta, window, turned, pairs)
    aq_in, kv_in = pl.pallas_call(
        leave_kernel,
        out_shape=[shape((GROUP, BLK, 128), bf)] * 2,
        in_specs=[VMEM] * 3,
        out_specs=[VMEM] * 2,
        scratch_shapes=[
            slabs, slabs, slabs, slabs, pltpu.VMEM((4, SEG, SEG), bf),
            *sems(16, 16, 16, 16, 16, 16),
        ],
        compiler_params=pltpu.CompilerParams(
            collective_id=1, has_side_effects=True, vmem_limit_bytes=16 * 2**20
        ),
        name="leave",
    )(aq, total, meta)
    return pl.pallas_call(
        finish_kernel,
        out_shape=[shape((BLK, 16 * DIM), bf)] * 4,
        in_specs=[VMEM] * 2,
        out_specs=[VMEM] * 4,
        compiler_params=pltpu.CompilerParams(vmem_limit_bytes=8 * 2**20),
        name="finish",
    )(aq_in, kv_in)


def solution(mesh):
    rows = P(("blk", "head"), None)
    return jax.shard_map(
        body,
        mesh=mesh,
        in_specs=(rows, rows, rows, rows, P("blk"), P("blk", None), P("blk")),
        out_specs=(rows, rows, rows, rows),
        check_vma=False,
    )
```

time: 61.5 us -> 57 us (0.927)
  the two profiles are of different devices: /device:TPU:27 before, /device:TPU:1 now
where the time goes in v3:
time: 57 us; the launch traced here: 56.9 us
  Pallas kernels  56.2 us (99%)
  between operations  0.66 us (1%)
    pallas_call x1, Pallas kernels, body(): pl.pallas_call(enter_kernel, out_shape=[shape((8 * SEG, 128), bf), shape(...  26.8 us
    pallas_call x1, Pallas kernels, body(): pl.pallas_call(leave_kernel, out_shape=[shape((GROUP, BLK, 128), bf)] * 2...  19.8 us
    pallas_call x1, Pallas kernels, body(): pl.pallas_call(attend_kernel, out_shape=[shape((4 * SEG, 128), bf), shape...  8.32 us
    pallas_call x1, Pallas kernels, body(): pl.pallas_call(finish_kernel, out_shape=[shape((BLK, 16 * DIM), bf)] * 4,...  1.26 us

profile of v3, /device:TPU:1, one launch (start us, length us, event | category | flops | bytes accessed | tf_op | source)
XLA Modules:
  0.0 56.9 jit_solution(288820832616139627)
XLA Ops:
  0.6 26.8 %enter.1 = (bf16[4096,128]{1,0:T(8,128)(2,1)S(1)}, bf16[4096,128]{1,0:T(8,128)(2,1)S(1)}, bf16[17,256,128]{2,1,0:T(8,128)(2,1)S(1)}, s32[4,16,128]{2,1,0:T(8,128)S(1)}) custom-call(bf16[128,1024]{1,0:T(8,128)(2,1)} %q_hbm.1, bf16[128,1024]{1,0:T(8,128)(2,1)} %k_hbm.1, bf16[128,1024]{1,0:T(8,128)(2,1)} %v_hbm.1, bf16[128,1024]{1,0:T(8,128)(2,1)} %g_hbm.1, ...), custom_call_target="tpu_custom_call" | custom-call | tf_op jit(solution)/shard_map/enter/pallas_call | solution.py:383
  27.4 8.3 %attend.1 = (bf16[2048,128]{1,0:T(8,128)(2,1)S(1)}, f32[4096,128]{1,0:T(8,128)S(1)}) custom-call(s32[4,16,128]{2,1,0:T(8,128)S(1)} %get-tuple-element.12.meta_ref, bf16[4096,128]{1,0:T(8,128)(2,1)S(1)} %get-tuple-element.13.window_ref, bf16[4096,128]{1,0:T(8,128)(2,1)S(1)} %get-tuple-element.14.turned_ref, bf16[17,256,128]{2,1,0:T(8,128)(2,1)S(1)} %get-tuple-element.15.pairs), custom_call_target="tpu_custom_call" | custom-call | tf_op jit(solution)/shard_map/attend/pallas_call | solution.py:415
  35.8 19.8 %leave.1 = (bf16[16,128,128]{2,1,0:T(8,128)(2,1)S(1)}, bf16[16,128,128]{2,1,0:T(8,128)(2,1)S(1)}) custom-call(bf16[2048,128]{1,0:T(8,128)(2,1)S(1)} %get-tuple-element.16.aq_ref, f32[4096,128]{1,0:T(8,128)S(1)} %get-tuple-element.17.total_ref, s32[4,16,128]{2,1,0:T(8,128)S(1)} %get-tuple-element.12.meta_ref), custom_call_target="tpu_custom_call" | custom-call | tf_op jit(solution)/shard_map/leave/pallas_call | solution.py:428
  55.6 1.3 %finish.1 = (bf16[128,1024]{1,0:T(8,128)(2,1)}, bf16[128,1024]{1,0:T(8,128)(2,1)}, bf16[128,1024]{1,0:T(8,128)(2,1)}, bf16[128,1024]{1,0:T(8,128)(2,1)}) custom-call(bf16[16,128,128]{2,1,0:T(8,128)(2,1)S(1)} %get-tuple-element.18.aq_ref, bf16[16,128,128]{2,1,0:T(8,128)(2,1)S(1)} %get-tuple-element.19.kv_ref), custom_call_target="tpu_custom_call" | custom-call | tf_op jit(solution)/shard_map/finish/pallas_call | solution.py:442

commit v4 on v3

--- a/solution.py
+++ b/solution.py
@@ -12,7 +12,8 @@
 SEG = 512
 DIM = 64
 LIST = 12
-UNROLL = 16
+UNROLL = 40
+REST = 8
 GROUP = 16
 NT = (((1,), (1,)), ((), ()))
 TN = (((0,), (0,)), ((), ()))
@@ -82,7 +83,7 @@
 
 def enter_kernel(
     q_hbm, k_hbm, v_hbm, g_hbm, order_hbm, lists_hbm, counts_hbm,
-    window_ref, turned_ref, pairs_ref, meta_ref,
+    window_ref, turned_ref, pairs_ref, meta_ref, table_ref,
     q_ref, k_ref, v_ref, g_ref, order_ref, lists_ref, counts_ref,
     kv_out, qg_out, kv_in, qg_in, halo_in, meta_in, meta_halo, picks,
     kv_ss, kv_rs, qg_ss, qg_rs, halo_ss, halo_rs, meta_ss, meta_rs, side_ss, side_rs, local_sem,
@@ -167,6 +168,10 @@
             picks[at, :, t * 128 : t * 128 + 128] = (order == lane + 128.0 * t).astype(jnp.bfloat16)
 
     meta_ref[...] = meta_in[...]
+    table_ref[...] = jnp.zeros((24, 128), jnp.int32)
+    for s in range(4):
+        table_ref[4 * s : 4 * s + 4, :] = meta_in[s, 4:8, :]
+        table_ref[16 + s : 17 + s, :] = meta_in[s, 8:9, :]
     for dx, dy, dc in OTHERS:
         slot = other(part, (-dx % 4, dy, dc))
         landed(kv_in, kv_rs, slot)
@@ -192,14 +197,15 @@
         keep(1024 + s * SEG, blocked(s, kv_in, s))
     for dx, dy, dc in OTHERS:
         landed(qg_in, qg_rs, other(part, (-dx % 4, dy, dc)))
-    for slot in range(GROUP):
-        landed(halo_in, halo_rs, slot)
     low = lax.broadcasted_iota(jnp.int32, (SEG, 128), 1) < DIM
     for s in range(4):
         qg = blocked(s, qg_in, s)
         zero = jnp.zeros_like(qg)
         pairs_ref[4 * s : 4 * s + 4, :BLK] = jnp.where(low, qg, zero).reshape(4, BLK, 128)
         pairs_ref[4 * s : 4 * s + 4, BLK:] = jnp.where(low, zero, qg).reshape(4, BLK, 128)
+    for slot in range(GROUP):
+        landed(halo_in, halo_rs, slot)
+    for s in range(4):
         keep((s if s < 2 else s + 4) * SEG, blocked(4 + s, halo_in, s))
     pairs_ref[16] = jnp.zeros((2 * BLK, 128), jnp.bfloat16)
     for copy in sends:
@@ -209,90 +215,93 @@
 
 
 def attend_kernel(
-    meta_ref, window_ref, turned_ref, pairs, aq_ref, total_ref,
-    block_of, first_of, second_of, whole_of, both, acc, top, mass, dot,
+    lists_ref, window_ref, turned_ref, pairs, aq_ref, total_ref,
+    code_of, part, change, high_of, acc, top, mass, dot,
 ):
     live = 0
     for b in range(16):
-        count = meta_ref[b // 4, 8, b % 4]
+        count = lists_ref[16 + b // 4, b % 4]
+        base = b // 4 * 4 * 33 + b * 1024
         for i in range(LIST // 2):
-            block_of[live + i] = b
-            first_of[live + i] = (b // 4 * 4 + meta_ref[b // 4, 4 + b % 4, 2 * i]) * BLK
-            second_of[live + i] = (b // 4 * 4 + meta_ref[b // 4, 4 + b % 4, 2 * i + 1]) * BLK
-            whole_of[live + i] = count - 2 * i - 1
+            code = lists_ref[b, 2 * i] + lists_ref[b, 2 * i + 1] * 32 + base
+            code_of[live + i] = jnp.where(count > 2 * i + 1, code + 32768, code)
         live = live + (count + 1) // 2
-    for u in range(UNROLL):
-        block_of[live + u] = 16
-        first_of[live + u] = 0
-        second_of[live + u] = BLK
-        whole_of[live + u] = 0
-    steps = (live + UNROLL - 1) // UNROLL
+    for u in range(REST):
+        code_of[live + u] = 16 * 1024 + 32
     total_ref[...] = jnp.zeros_like(total_ref)
     acc[...] = jnp.zeros_like(acc)
     top[...] = jnp.full(top.shape, -jnp.inf, jnp.float32)
     mass[...] = jnp.zeros_like(mass)
     dot[...] = jnp.zeros_like(dot)
 
-    def tiles(step, u):
-        t = step * UNROLL + u
-        spans = [pl.ds(pl.multiple_of(ref[t], BLK), BLK) for ref in (first_of, second_of)]
-        return t, block_of[t], spans[0], spans[1], whole_of[t] > 0
+    def tiles(t):
+        code = code_of[t]
+        spans = [pl.ds(pl.multiple_of((code // at % 32) * BLK, BLK), BLK) for at in (1, 32)]
+        return code // 1024 % 32, spans[0], spans[1], code >= 32768
 
     def lay(x):
-        return x.reshape(BLK // 8, 8, 128)
-
-    def scores(step, carry):
-        for u in range(UNROLL):
-            t, b, one, two, whole = tiles(step, u)
-            kv = jnp.concatenate([window_ref[one, :], window_ref[two, :]], axis=0)
-            out = lax.dot_general(kv, pairs[b], NT, preferred_element_type=jnp.float32)
-            both[t] = out
-            high = jnp.max(lay(out[:BLK, :BLK]), axis=0)
-            other_high = jnp.max(lay(out[BLK:, :BLK]), axis=0)
-            high = jnp.maximum(high, jnp.where(whole, other_high, -jnp.inf))
-            top[b] = jnp.maximum(top[b], high)
-        return carry
-
-    lax.fori_loop(0, steps, scores, 0)
-    top[...] = jnp.broadcast_to(jnp.max(top[...], axis=1, keepdims=True) * LOG2E, top.shape)
-
-    def weigh(step, carry):
-        for u in range(UNROLL):
-            t, b, _, _, whole = tiles(step, u)
-            high = top[b]
-            one = jnp.exp2(lay(both[t, :BLK, :BLK]) * LOG2E - high)
-            two = jnp.exp2(lay(both[t, BLK:, :BLK]) * LOG2E - jnp.where(whole, high, jnp.inf))
-            both[t, :BLK, :BLK] = one.reshape(BLK, BLK)
-            both[t, BLK:, :BLK] = two.reshape(BLK, BLK)
-            mass[b] = mass[b] + jnp.sum(one + two, axis=0)
-            dot[b] = dot[b] + jnp.sum(
-                one * lay(both[t, :BLK, BLK:]) + two * lay(both[t, BLK:, BLK:]), axis=0
-            )
-        return carry
-
-    lax.fori_loop(0, steps, weigh, 0)
-    share = 1.0 / jnp.sum(mass[...], axis=1, keepdims=True)
-    dot[...] = jnp.broadcast_to(jnp.sum(dot[...], axis=1, keepdims=True) * share, dot.shape)
+        return x.reshape(-1, 8, 128)
+
+    def scores(t):
+        b, one, two, whole = tiles(t)
+        kv = jnp.concatenate([window_ref[one, :], window_ref[two, :]], axis=0)
+        out = lax.dot_general(kv, pairs[b], NT, preferred_element_type=jnp.float32)
+        one, two = lay(out[:BLK, :BLK]) * LOG2E, lay(out[BLK:, :BLK]) * LOG2E
+        other_high = jnp.where(whole, jnp.max(two, axis=0), -jnp.inf)
+        old = top[b]
+        high = jnp.maximum(old, jnp.maximum(jnp.max(one, axis=0), other_high))
+        top[b] = high
+        high_of[t] = high
+        one = jnp.exp2(one - high)
+        two = jnp.exp2(two - jnp.where(whole, high, jnp.inf))
+        part[t, :BLK] = one.reshape(BLK, BLK)
+        part[t, BLK:] = two.reshape(BLK, BLK)
+        change[t] = out[:, BLK:]
+        fade = jnp.exp2(old - high)
+        mass[b] = mass[b] * fade + jnp.sum(one + two, axis=0)
+        dot[b] = dot[b] * fade + jnp.sum(
+            one * lay(out[:BLK, BLK:]) + two * lay(out[BLK:, BLK:]), axis=0
+        )
+
+    def each(step):
+        many = live // UNROLL
+        few = (live - many * UNROLL + REST - 1) // REST
+
+        def run(start, count):
+            def several(i, carry):
+                for u in range(count):
+                    step(start + i * count + u)
+                return carry
+
+            return several
+
+        lax.fori_loop(0, many, run(0, UNROLL), 0)
+        lax.fori_loop(0, few, run(many * UNROLL, REST), 0)
+
+    each(scores)
+    highest = jnp.max(top[...], axis=1, keepdims=True)
+    fade = jnp.exp2(top[...] - highest)
+    share = 1.0 / jnp.sum(mass[...] * fade, axis=1, keepdims=True)
+    dot[...] = jnp.broadcast_to(jnp.sum(dot[...] * fade, axis=1, keepdims=True) * share, dot.shape)
     mass[...] = jnp.broadcast_to(share, mass.shape)
-
-    def grads(step, carry):
-        for u in range(UNROLL):
-            t, b, one, two, _ = tiles(step, u)
-            chance = both[t, :, :BLK].reshape(BLK // 4, 8, 128) * mass[b]
-            grad = chance * (both[t, :, BLK:].reshape(BLK // 4, 8, 128) - dot[b])
-            w = jnp.concatenate([grad.reshape(2 * BLK, BLK), chance.reshape(2 * BLK, BLK)], axis=1)
-            w = w.astype(jnp.bfloat16)
-            kv = jnp.concatenate([turned_ref[one, :], turned_ref[two, :]], axis=1)
-            out = jnp.dot(kv, w, preferred_element_type=jnp.float32)
-            acc[b, :DIM] = acc[b, :DIM] + out[:DIM, :BLK]
-            acc[b, DIM:] = acc[b, DIM:] + out[DIM:, BLK:]
-            out = jnp.dot(w, pairs[b], preferred_element_type=jnp.float32)
-            one_sum, two_sum = total_ref[one, :] + out[:BLK], total_ref[two, :] + out[BLK:]
-            total_ref[one, :] = one_sum
-            total_ref[two, :] = two_sum
-        return carry
-
-    lax.fori_loop(0, steps, grads, 0)
+    top[...] = jnp.broadcast_to(highest, top.shape)
+
+    def grads(t):
+        b, one, two, _ = tiles(t)
+        chance = lay(part[t]) * (jnp.exp2(high_of[t] - top[b]) * mass[b])
+        grad = chance * (lay(change[t]) - dot[b])
+        w = jnp.concatenate([grad.reshape(2 * BLK, BLK), chance.reshape(2 * BLK, BLK)], axis=1)
+        w = w.astype(jnp.bfloat16)
+        kv = jnp.concatenate([turned_ref[one, :], turned_ref[two, :]], axis=1)
+        out = jnp.dot(kv, w, preferred_element_type=jnp.float32)
+        acc[b, :DIM] = acc[b, :DIM] + out[:DIM, :BLK]
+        acc[b, DIM:] = acc[b, DIM:] + out[DIM:, BLK:]
+        out = jnp.dot(w, pairs[b], preferred_element_type=jnp.float32)
+        one_sum, two_sum = total_ref[one, :] + out[:BLK], total_ref[two, :] + out[BLK:]
+        total_ref[one, :] = one_sum
+        total_ref[two, :] = two_sum
+
+    each(grads)
     for b in range(16):
         out = jnp.concatenate([acc[b, :DIM] * SCALE, acc[b, DIM:]], axis=0).astype(jnp.bfloat16)
         aq_ref[b * BLK : b * BLK + BLK, :] = jnp.transpose(out)
@@ -361,13 +370,20 @@
                 remote(there, there, ssem.at[slot], rsem.at[slot], left).wait_recv()
 
 
-def finish_kernel(aq_ref, kv_ref, out_ref, dq_ref, dk_ref, dv_ref):
-    for arrived, low_ref, high_ref in ((aq_ref, dq_ref, out_ref), (kv_ref, dk_ref, dv_ref)):
+def finish_kernel(aq_ref, kv_ref, *refs):
+    outs, made, sem = refs[:4], refs[4:8], refs[8]
+    copies = []
+    for i, arrived in ((0, aq_ref), (2, kv_ref)):
         for t in range(8):
             cols = slice(t * 128, t * 128 + 128)
             a, b = arrived[2 * t], arrived[2 * t + 1]
-            low_ref[:, cols] = jnp.concatenate([a[:, :DIM], b[:, :DIM]], axis=1)
-            high_ref[:, cols] = jnp.concatenate([a[:, DIM:], b[:, DIM:]], axis=1)
+            made[i][:, cols] = jnp.concatenate([a[:, DIM:], b[:, DIM:]], axis=1)
+            made[i + 1][:, cols] = jnp.concatenate([a[:, :DIM], b[:, :DIM]], axis=1)
+        for j in (i, i + 1):
+            copies.append(pltpu.make_async_copy(made[j], outs[j], sem.at[j]))
+            copies[-1].start()
+    for copy in copies:
+        copy.wait()
 
 
 def sems(*counts):
@@ -380,16 +396,17 @@
     slabs = pltpu.VMEM((GROUP, BLK, 128), bf)
     numbers = pltpu.VMEM((4, 16, 128), i32)
     mine = pltpu.VMEM((BLK, 16 * DIM), bf)
-    window, turned, pairs, meta = pl.pallas_call(
+    window, turned, pairs, meta, lists = pl.pallas_call(
         enter_kernel,
         out_shape=[
             shape((8 * SEG, 128), bf),
             shape((8 * SEG, 128), bf),
             shape((17, 2 * BLK, 128), bf),
             shape((4, 16, 128), i32),
+            shape((24, 128), i32),
         ],
         in_specs=[HBM] * 7,
-        out_specs=[VMEM] * 4,
+        out_specs=[VMEM] * 5,
         scratch_shapes=[
             mine, mine, mine, mine,
             pltpu.VMEM((1, SEG), i32), pltpu.VMEM((4, LIST), i32), pltpu.VMEM((1, 4), i32),
@@ -410,21 +427,21 @@
         )
     )
     stats = pltpu.VMEM((17, 8, 128), f32)
-    pairs_most = 8 * LIST + 16
-    table = pltpu.SMEM((pairs_most,), i32)
+    pairs_most = 8 * LIST + 8
+    tiles = pltpu.VMEM((pairs_most, 2 * BLK, BLK), f32)
     aq, total = pl.pallas_call(
         attend_kernel,
         out_shape=[shape((4 * SEG, 128), bf), shape((8 * SEG, 128), f32)],
         in_specs=[SMEM, VMEM, VMEM, VMEM],
         out_specs=[VMEM] * 2,
         scratch_shapes=[
-            table, table, table, table,
-            pltpu.VMEM((pairs_most, 2 * BLK, 2 * BLK), f32), pltpu.VMEM((17, 128, BLK), f32),
+            pltpu.SMEM((pairs_most,), i32),
+            tiles, tiles, pltpu.VMEM((pairs_most, 8, 128), f32), pltpu.VMEM((17, 128, BLK), f32),
             stats, stats, stats,
         ],
         compiler_params=pltpu.CompilerParams(vmem_limit_bytes=40 * 2**20),
         name="attend",
-    )(meta, window, turned, pairs)
+    )(lists, window, turned, pairs)
     aq_in, kv_in = pl.pallas_call(
         leave_kernel,
         out_shape=[shape((GROUP, BLK, 128), bf)] * 2,
@@ -439,14 +456,16 @@
         ),
         name="leave",
     )(aq, total, meta)
-    return pl.pallas_call(
+    out, dq, dv, dk = pl.pallas_call(
         finish_kernel,
         out_shape=[shape((BLK, 16 * DIM), bf)] * 4,
         in_specs=[VMEM] * 2,
-        out_specs=[VMEM] * 4,
+        out_specs=[HBM] * 4,
+        scratch_shapes=[mine, mine, mine, mine, *sems(4)],
         compiler_params=pltpu.CompilerParams(vmem_limit_bytes=8 * 2**20),
         name="finish",
     )(aq_in, kv_in)
+    return out, dq, dk, dv
 
 
 def solution(mesh):

time: 57 us -> 55.7 us (0.977)
  Pallas kernels: 56.2 us -> 54.8 us
    pallas_call x1, Pallas kernels: 8.32 us -> 7.47 us  [body(): pl.pallas_call(attend_kernel, out_shape=[shape((4 * SEG, 128), bf), shape...]
    pallas_call x1, Pallas kernels: 19.8 us -> 19.1 us  [body(): pl.pallas_call(leave_kernel, out_shape=[shape((GROUP, BLK, 128), bf)] * 2...]
where the time goes in v4:
time: 55.7 us; the launch traced here: 55.6 us
  Pallas kernels  54.8 us (98%)
  between operations  0.82 us (1%)
    pallas_call x1, Pallas kernels, body(): pl.pallas_call(enter_kernel, out_shape=[shape((8 * SEG, 128), bf), shape(...  27 us
    pallas_call x1, Pallas kernels, body(): pl.pallas_call(leave_kernel, out_shape=[shape((GROUP, BLK, 128), bf)] * 2...  19.1 us
    pallas_call x1, Pallas kernels, body(): pl.pallas_call(attend_kernel, out_shape=[shape((4 * SEG, 128), bf), shape...  7.47 us
    pallas_call x1, Pallas kernels, body(): pl.pallas_call(finish_kernel, out_shape=[shape((BLK, 16 * DIM), bf)] * 4,...  1.21 us

profile of v4, /device:TPU:1, one launch (start us, length us, event | category | flops | bytes accessed | tf_op | source)
XLA Modules:
  0.0 55.6 jit_solution(2722692964757037310)
XLA Ops:
  0.6 27.0 %enter.1 = (bf16[4096,128]{1,0:T(8,128)(2,1)S(1)}, bf16[4096,128]{1,0:T(8,128)(2,1)S(1)}, bf16[17,256,128]{2,1,0:T(8,128)(2,1)S(1)}, s32[4,16,128]{2,1,0:T(8,128)S(1)}, s32[24,128]{1,0:T(8,128)S(1)}) custom-call(bf16[128,1024]{1,0:T(8,128)(2,1)} %q_hbm.1, bf16[128,1024]{1,0:T(8,128)(2,1)} %k_hbm.1, bf16[128,1024]{1,0:T(8,128)(2,1)} %v_hbm.1, ...), custom_call_target="tpu_custom_call" | custom-call | tf_op jit(solution)/shard_map/enter/pallas_call | solution.py:399
  27.6 7.5 %attend.1 = (bf16[2048,128]{1,0:T(8,128)(2,1)S(1)}, f32[4096,128]{1,0:T(8,128)S(1)}) custom-call(s32[24,128]{1,0:T(8,128)S(1)} %get-tuple-element.17.lists_ref, bf16[4096,128]{1,0:T(8,128)(2,1)S(1)} %get-tuple-element.18.window_ref, bf16[4096,128]{1,0:T(8,128)(2,1)S(1)} %get-tuple-element.19.turned_ref, bf16[17,256,128]{2,1,0:T(8,128)(2,1)S(1)} %get-tuple-element.20.pairs), custom_call_target="tpu_custom_call" | custom-call | tf_op jit(solution)/shard_map/attend/pallas_call | solution.py:432
  35.1 19.1 %leave.1 = (bf16[16,128,128]{2,1,0:T(8,128)(2,1)S(1)}, bf16[16,128,128]{2,1,0:T(8,128)(2,1)S(1)}) custom-call(bf16[2048,128]{1,0:T(8,128)(2,1)S(1)} %get-tuple-element.21.aq_ref, f32[4096,128]{1,0:T(8,128)S(1)} %get-tuple-element.22.total_ref, s32[4,16,128]{2,1,0:T(8,128)S(1)} %get-tuple-element.23.meta_ref), custom_call_target="tpu_custom_call" | custom-call | tf_op jit(solution)/shard_map/leave/pallas_call | solution.py:445
  54.2 1.2 %finish.1 = (bf16[128,1024]{1,0:T(8,128)(2,1)}, bf16[128,1024]{1,0:T(8,128)(2,1)}, bf16[128,1024]{1,0:T(8,128)(2,1)}, bf16[128,1024]{1,0:T(8,128)(2,1)}) custom-call(bf16[16,128,128]{2,1,0:T(8,128)(2,1)S(1)} %get-tuple-element.24.aq_ref, bf16[16,128,128]{2,1,0:T(8,128)(2,1)S(1)} %get-tuple-element.25.kv_ref), custom_call_target="tpu_custom_call" | custom-call | tf_op jit(solution)/shard_map/finish/pallas_call | solution.py:459

commit v5 on v4

--- a/solution.py
+++ b/solution.py
@@ -18,7 +18,6 @@
 NT = (((1,), (1,)), ((), ()))
 TN = (((0,), (0,)), ((), ()))
 SCALE = 1.0 / math.sqrt(DIM)
-LOG2E = math.log2(math.e)
 MESH = pl.DeviceIdType.MESH
 HBM = pl.BlockSpec(memory_space=pltpu.HBM)
 VMEM = pl.BlockSpec(memory_space=pltpu.VMEM)
@@ -236,8 +235,8 @@
 
     def tiles(t):
         code = code_of[t]
-        spans = [pl.ds(pl.multiple_of((code // at % 32) * BLK, BLK), BLK) for at in (1, 32)]
-        return code // 1024 % 32, spans[0], spans[1], code >= 32768
+        spans = [pl.ds(pl.multiple_of(((code >> at) & 31) * BLK, BLK), BLK) for at in (0, 5)]
+        return (code >> 10) & 31, spans[0], spans[1], code >= 32768
 
     def lay(x):
         return x.reshape(-1, 8, 128)
@@ -246,18 +245,18 @@
         b, one, two, whole = tiles(t)
         kv = jnp.concatenate([window_ref[one, :], window_ref[two, :]], axis=0)
         out = lax.dot_general(kv, pairs[b], NT, preferred_element_type=jnp.float32)
-        one, two = lay(out[:BLK, :BLK]) * LOG2E, lay(out[BLK:, :BLK]) * LOG2E
+        one, two = lay(out[:BLK, :BLK]), lay(out[BLK:, :BLK])
         other_high = jnp.where(whole, jnp.max(two, axis=0), -jnp.inf)
         old = top[b]
         high = jnp.maximum(old, jnp.maximum(jnp.max(one, axis=0), other_high))
         top[b] = high
         high_of[t] = high
-        one = jnp.exp2(one - high)
-        two = jnp.exp2(two - jnp.where(whole, high, jnp.inf))
+        one = jnp.exp(one - high)
+        two = jnp.exp(two - jnp.where(whole, high, jnp.inf))
         part[t, :BLK] = one.reshape(BLK, BLK)
         part[t, BLK:] = two.reshape(BLK, BLK)
         change[t] = out[:, BLK:]
-        fade = jnp.exp2(old - high)
+        fade = jnp.exp(old - high)
         mass[b] = mass[b] * fade + jnp.sum(one + two, axis=0)
         dot[b] = dot[b] * fade + jnp.sum(
             one * lay(out[:BLK, BLK:]) + two * lay(out[BLK:, BLK:]), axis=0
@@ -280,7 +279,7 @@
 
     each(scores)
     highest = jnp.max(top[...], axis=1, keepdims=True)
-    fade = jnp.exp2(top[...] - highest)
+    fade = jnp.exp(top[...] - highest)
     share = 1.0 / jnp.sum(mass[...] * fade, axis=1, keepdims=True)
     dot[...] = jnp.broadcast_to(jnp.sum(dot[...] * fade, axis=1, keepdims=True) * share, dot.shape)
     mass[...] = jnp.broadcast_to(share, mass.shape)
@@ -288,7 +287,7 @@
 
     def grads(t):
         b, one, two, _ = tiles(t)
-        chance = lay(part[t]) * (jnp.exp2(high_of[t] - top[b]) * mass[b])
+        chance = lay(part[t]) * (jnp.exp(high_of[t] - top[b]) * mass[b])
         grad = chance * (lay(change[t]) - dot[b])
         w = jnp.concatenate([grad.reshape(2 * BLK, BLK), chance.reshape(2 * BLK, BLK)], axis=1)
         w = w.astype(jnp.bfloat16)
@@ -334,11 +333,11 @@
         here = lax.rem(there + 8, GROUP)
         device = [jnp.where(here < 8, a, b) for a, b in zip(left, right)]
         remote(halo_out.at[here], halo_in.at[there], halo_ss.at[here], halo_rs.at[there], device).start()
-        if i < len(OTHERS):
-            slot = other(part, OTHERS[i])
-            remote(
-                aq_nat.at[slot], aq_in.at[role], aq_ss.at[slot], aq_rs.at[role], member(quad, slot)
-            ).start()
+    for steps in OTHERS:
+        slot = other(part, steps)
+        remote(
+            aq_nat.at[slot], aq_in.at[role], aq_ss.at[slot], aq_rs.at[role], member(quad, slot)
+        ).start()
     aq_in[role] = aq_nat[part]
     for s, dx in zip(turn, (2, 1, 3, 0)):
         for p in range(4):

time: 55.7 us -> 55.8 us (level)
    pallas_call x1, Pallas kernels: 19.1 us -> 21 us  [body(): pl.pallas_call(leave_kernel, out_shape=[shape((GROUP, BLK, 128), bf)] * 2...]
    pallas_call x1, Pallas kernels: 7.47 us -> 6.03 us  [body(): pl.pallas_call(attend_kernel, out_shape=[shape((4 * SEG, 128), bf), shape...]
where the time goes in v5:
time: 55.8 us; the launch traced here: 56 us
  Pallas kernels  55.2 us (99%)
  between operations  0.82 us (1%)
    pallas_call x1, Pallas kernels, body(): pl.pallas_call(enter_kernel, out_shape=[shape((8 * SEG, 128), bf), shape(...  27 us
    pallas_call x1, Pallas kernels, body(): pl.pallas_call(leave_kernel, out_shape=[shape((GROUP, BLK, 128), bf)] * 2...  21 us
    pallas_call x1, Pallas kernels, body(): pl.pallas_call(attend_kernel, out_shape=[shape((4 * SEG, 128), bf), shape...  6.03 us
    pallas_call x1, Pallas kernels, body(): pl.pallas_call(finish_kernel, out_shape=[shape((BLK, 16 * DIM), bf)] * 4,...  1.21 us

profile of v5, /device:TPU:1, one launch (start us, length us, event | category | flops | bytes accessed | tf_op | source)
XLA Modules:
  0.0 56.0 jit_solution(14341067658887398575)
XLA Ops:
  0.6 27.0 %enter.1 = (bf16[4096,128]{1,0:T(8,128)(2,1)S(1)}, bf16[4096,128]{1,0:T(8,128)(2,1)S(1)}, bf16[17,256,128]{2,1,0:T(8,128)(2,1)S(1)}, s32[4,16,128]{2,1,0:T(8,128)S(1)}, s32[24,128]{1,0:T(8,128)S(1)}) custom-call(bf16[128,1024]{1,0:T(8,128)(2,1)} %q_hbm.1, bf16[128,1024]{1,0:T(8,128)(2,1)} %k_hbm.1, bf16[128,1024]{1,0:T(8,128)(2,1)} %v_hbm.1, ...), custom_call_target="tpu_custom_call" | custom-call | tf_op jit(solution)/shard_map/enter/pallas_call | solution.py:398
  27.6 6.0 %attend.1 = (bf16[2048,128]{1,0:T(8,128)(2,1)S(1)}, f32[4096,128]{1,0:T(8,128)S(1)}) custom-call(s32[24,128]{1,0:T(8,128)S(1)} %get-tuple-element.17.lists_ref, bf16[4096,128]{1,0:T(8,128)(2,1)S(1)} %get-tuple-element.18.window_ref, bf16[4096,128]{1,0:T(8,128)(2,1)S(1)} %get-tuple-element.19.turned_ref, bf16[17,256,128]{2,1,0:T(8,128)(2,1)S(1)} %get-tuple-element.20.pairs), custom_call_target="tpu_custom_call" | custom-call | tf_op jit(solution)/shard_map/attend/pallas_call | solution.py:431
  33.7 21.0 %leave.1 = (bf16[16,128,128]{2,1,0:T(8,128)(2,1)S(1)}, bf16[16,128,128]{2,1,0:T(8,128)(2,1)S(1)}) custom-call(bf16[2048,128]{1,0:T(8,128)(2,1)S(1)} %get-tuple-element.21.aq_ref, f32[4096,128]{1,0:T(8,128)S(1)} %get-tuple-element.22.total_ref, s32[4,16,128]{2,1,0:T(8,128)S(1)} %get-tuple-element.23.meta_ref), custom_call_target="tpu_custom_call" | custom-call | tf_op jit(solution)/shard_map/leave/pallas_call | solution.py:444
  54.6 1.2 %finish.1 = (bf16[128,1024]{1,0:T(8,128)(2,1)}, bf16[128,1024]{1,0:T(8,128)(2,1)}, bf16[128,1024]{1,0:T(8,128)(2,1)}, bf16[128,1024]{1,0:T(8,128)(2,1)}) custom-call(bf16[16,128,128]{2,1,0:T(8,128)(2,1)S(1)} %get-tuple-element.24.aq_ref, bf16[16,128,128]{2,1,0:T(8,128)(2,1)S(1)} %get-tuple-element.25.kv_ref), custom_call_target="tpu_custom_call" | custom-call | tf_op jit(solution)/shard_map/finish/pallas_call | solution.py:458

commit v6 on v5

--- a/solution.py
+++ b/solution.py
@@ -13,6 +13,7 @@
 DIM = 64
 LIST = 12
 UNROLL = 40
+MIDDLE = 16
 REST = 8
 GROUP = 16
 NT = (((1,), (1,)), ((), ()))
@@ -264,7 +265,9 @@
 
     def each(step):
         many = live // UNROLL
-        few = (live - many * UNROLL + REST - 1) // REST
+        some = (live - many * UNROLL) // MIDDLE
+        done = many * UNROLL + some * MIDDLE
+        few = (live - done + REST - 1) // REST
 
         def run(start, count):
             def several(i, carry):
@@ -275,7 +278,8 @@
             return several
 
         lax.fori_loop(0, many, run(0, UNROLL), 0)
-        lax.fori_loop(0, few, run(many * UNROLL, REST), 0)
+        lax.fori_loop(0, some, run(many * UNROLL, MIDDLE), 0)
+        lax.fori_loop(0, few, run(done, REST), 0)
 
     each(scores)
     highest = jnp.max(top[...], axis=1, keepdims=True)

time: 55.8 us -> 55.3 us (level); the launches traced: 56 us -> 54.9 us
  Pallas kernels: 55.2 us -> 54.1 us
    pallas_call x1, Pallas kernels: 21 us -> 19.1 us  [body(): pl.pallas_call(leave_kernel, out_shape=[shape((GROUP, BLK, 128), bf)] * 2...]
    pallas_call x1, Pallas kernels: 6.03 us -> 6.76 us  [body(): pl.pallas_call(attend_kernel, out_shape=[shape((4 * SEG, 128), bf), shape...]
where the time goes in v6:
time: 55.3 us; the launch traced here: 54.9 us
  Pallas kernels  54.1 us (98%)
  between operations  0.82 us (1%)
    pallas_call x1, Pallas kernels, body(): pl.pallas_call(enter_kernel, out_shape=[shape((8 * SEG, 128), bf), shape(...  27 us
    pallas_call x1, Pallas kernels, body(): pl.pallas_call(leave_kernel, out_shape=[shape((GROUP, BLK, 128), bf)] * 2...  19.1 us
    pallas_call x1, Pallas kernels, body(): pl.pallas_call(attend_kernel, out_shape=[shape((4 * SEG, 128), bf), shape...  6.76 us
    pallas_call x1, Pallas kernels, body(): pl.pallas_call(finish_kernel, out_shape=[shape((BLK, 16 * DIM), bf)] * 4,...  1.21 us

profile of v6, /device:TPU:1, one launch (start us, length us, event | category | flops | bytes accessed | tf_op | source)
XLA Modules:
  0.0 54.9 jit_solution(16671100366857945592)
XLA Ops:
  0.6 27.0 %enter.1 = (bf16[4096,128]{1,0:T(8,128)(2,1)S(1)}, bf16[4096,128]{1,0:T(8,128)(2,1)S(1)}, bf16[17,256,128]{2,1,0:T(8,128)(2,1)S(1)}, s32[4,16,128]{2,1,0:T(8,128)S(1)}, s32[24,128]{1,0:T(8,128)S(1)}) custom-call(bf16[128,1024]{1,0:T(8,128)(2,1)} %q_hbm.1, bf16[128,1024]{1,0:T(8,128)(2,1)} %k_hbm.1, bf16[128,1024]{1,0:T(8,128)(2,1)} %v_hbm.1, ...), custom_call_target="tpu_custom_call" | custom-call | tf_op jit(solution)/shard_map/enter/pallas_call | solution.py:402
  27.6 6.8 %attend.1 = (bf16[2048,128]{1,0:T(8,128)(2,1)S(1)}, f32[4096,128]{1,0:T(8,128)S(1)}) custom-call(s32[24,128]{1,0:T(8,128)S(1)} %get-tuple-element.17.lists_ref, bf16[4096,128]{1,0:T(8,128)(2,1)S(1)} %get-tuple-element.18.window_ref, bf16[4096,128]{1,0:T(8,128)(2,1)S(1)} %get-tuple-element.19.turned_ref, bf16[17,256,128]{2,1,0:T(8,128)(2,1)S(1)} %get-tuple-element.20.pairs), custom_call_target="tpu_custom_call" | custom-call | tf_op jit(solution)/shard_map/attend/pallas_call | solution.py:435
  34.4 19.1 %leave.1 = (bf16[16,128,128]{2,1,0:T(8,128)(2,1)S(1)}, bf16[16,128,128]{2,1,0:T(8,128)(2,1)S(1)}) custom-call(bf16[2048,128]{1,0:T(8,128)(2,1)S(1)} %get-tuple-element.21.aq_ref, f32[4096,128]{1,0:T(8,128)S(1)} %get-tuple-element.22.total_ref, s32[4,16,128]{2,1,0:T(8,128)S(1)} %get-tuple-element.23.meta_ref), custom_call_target="tpu_custom_call" | custom-call | tf_op jit(solution)/shard_map/leave/pallas_call | solution.py:448
  53.5 1.2 %finish.1 = (bf16[128,1024]{1,0:T(8,128)(2,1)}, bf16[128,1024]{1,0:T(8,128)(2,1)}, bf16[128,1024]{1,0:T(8,128)(2,1)}, bf16[128,1024]{1,0:T(8,128)(2,1)}) custom-call(bf16[16,128,128]{2,1,0:T(8,128)(2,1)S(1)} %get-tuple-element.24.aq_ref, bf16[16,128,128]{2,1,0:T(8,128)(2,1)S(1)} %get-tuple-element.25.kv_ref), custom_call_target="tpu_custom_call" | custom-call | tf_op jit(solution)/shard_map/finish/pallas_call | solution.py:462
